TPU v7x, 256 devices: a whole 4x4x8 slice. The times are simulated.
256 devices in a mesh: dp: 16 (over x, y), expert: 16 (over z, core).
Axes of the slice: x: 4, y: 4, z: 8, core: 2. Of those that a mesh axis runs over, the one named last changes fastest.
Arguments:
- tokens: bfloat16 [40960, 2048], P(('dp', 'expert')), may hold values from -24 to 24
- out_grads: bfloat16 [40960, 2048], P(('dp', 'expert')), may hold values from -6 to 6
- expert_ids: int32 [40960, 1], P(('dp', 'expert')), may hold values from 0 to 15; in each aligned block of 160 rows (0 to 159, 160 to 319, ...) at most 30 rows name the same one
- w_gate_up: bfloat16 [16, 2048, 1536], P('expert'), may hold values from -0.125 to 0.125
- w_down_t: bfloat16 [16, 2048, 768], P('expert'), may hold values from -0.21875 to 0.21875
Outputs:
- token_grads: bfloat16 [40960, 2048], P(('dp', 'expert'))
- grad_gate_up: bfloat16 [16, 2048, 1536], P('expert', 'dp')
- grad_down_t: bfloat16 [16, 2048, 768], P('expert', 'dp')
Inputs may be any that keep to these rules, and one draw needn't show every extreme that they name: `expert_ids`: within one device's 160 rows (an aligned block) no expert is named more than 30 times; in some blocks one expert is named exactly 30 times.
All inputs are finite; a program needn't handle non-finite values.
Results may differ from a plain program's by a relative error of at most 0.02.
Values may be sent and summed in bfloat16 or wider, within the bound.
No kernel may reach another device: no remote copies, remote signals or barrier semaphores. Data moves between devices by JAX's collectives and lax.ppermute only.
A program may use at most 128 MiB of HBM per device.

v0:
```python
import jax
import jax.numpy as jnp
from jax import lax
from jax.sharding import PartitionSpec as P


def slot_table(routed, num_experts, capacity):
    onehot = (routed[:, None] == jnp.arange(num_experts, dtype=jnp.int32)[None, :]).astype(
        jnp.int32
    )
    ranks = jnp.cumsum(onehot, axis=0) - 1
    slots = jnp.sum(ranks * onehot, axis=1)
    target = routed * capacity + slots
    places = jnp.arange(num_experts * capacity, dtype=jnp.int32)
    return (places[:, None] == target[None, :]).astype(jnp.bfloat16)


def local(tokens, out_grads, expert_ids, w_gate_up, w_down_t):
    tok_rows = tokens.shape[0]
    width = tokens.shape[1]
    num_experts = lax.axis_size("expert")
    capacity = 3 * tok_rows // num_experts
    hidden_units = w_down_t.shape[2]
    routed = expert_ids[:, 0]
    dispatch = slot_table(routed, num_experts, capacity)
    all_x, all_dy, all_ids = (
        lax.all_gather(tokens, "expert", axis=0, tiled=True),
        lax.all_gather(out_grads, "expert", axis=0, tiled=True),
        lax.all_gather(routed.astype(jnp.bfloat16), "expert", axis=0, tiled=True),
    )
    owner = lax.axis_index("expert")
    source_ids = all_ids.astype(jnp.int32).reshape(num_experts, tok_rows)
    mine = (source_ids == owner).astype(jnp.int32)
    ranks = jnp.cumsum(mine, axis=1) - 1
    slot_range = jnp.arange(capacity, dtype=jnp.int32)
    select = ((mine[:, None, :] == 1) & (ranks[:, None, :] == slot_range[None, :, None])).astype(
        jnp.bfloat16
    )
    rows_x = jnp.einsum(
        "jct,jtd->jcd",
        select,
        all_x.reshape(num_experts, tok_rows, width),
        preferred_element_type=jnp.float32,
    )
    rows_x = rows_x.reshape(num_experts * capacity, width).astype(jnp.bfloat16)
    rows_dy = jnp.einsum(
        "jct,jtd->jcd",
        select,
        all_dy.reshape(num_experts, tok_rows, width),
        preferred_element_type=jnp.float32,
    )
    rows_dy = rows_dy.reshape(num_experts * capacity, width).astype(jnp.bfloat16)
    weight_in = w_gate_up[0]
    weight_out = w_down_t[0]
    gate_up = jnp.dot(rows_x, weight_in, preferred_element_type=jnp.float32)
    gate = gate_up[:, :hidden_units]
    upper = gate_up[:, hidden_units:]
    sigmoid_gate = jax.nn.sigmoid(gate)
    silu_gate = gate * sigmoid_gate
    hidden = (silu_gate * upper).astype(jnp.bfloat16)
    dhidden = jnp.dot(rows_dy, weight_out, preferred_element_type=jnp.float32)
    dgate = dhidden * upper * sigmoid_gate * (1.0 + gate * (1.0 - sigmoid_gate))
    dupper = dhidden * silu_gate
    dgate_up = jnp.concatenate([dgate, dupper], axis=1).astype(jnp.bfloat16)
    drows = lax.dot_general(
        dgate_up, weight_in, (((1,), (1,)), ((), ())), preferred_element_type=jnp.float32
    ).astype(jnp.bfloat16)
    returned = lax.all_to_all(drows, "expert", split_axis=0, concat_axis=0, tiled=True)
    token_grads = lax.dot_general(
        dispatch, returned, (((0,), (0,)), ((), ())), preferred_element_type=jnp.float32
    ).astype(jnp.bfloat16)
    first = lax.dot_general(
        rows_x, dgate_up, (((0,), (0,)), ((), ())), preferred_element_type=jnp.float32
    )
    second = lax.dot_general(
        rows_dy, hidden, (((0,), (0,)), ((), ())), preferred_element_type=jnp.float32
    )
    summed = lax.psum_scatter(
        jnp.concatenate([first, second], axis=1).astype(jnp.bfloat16),
        "dp",
        scatter_dimension=0,
        tiled=True,
    ).astype(jnp.float32)
    grad_gate_up = summed[:, : 2 * hidden_units].astype(jnp.bfloat16)[None]
    grad_down_t = summed[:, 2 * hidden_units :].astype(jnp.bfloat16)[None]
    return (token_grads, grad_gate_up, grad_down_t)


def solution(mesh):
    return jax.shard_map(
        local,
        mesh=mesh,
        in_specs=(
            P(("dp", "expert"), None),
            P(("dp", "expert"), None),
            P(("dp", "expert"), None),
            P("expert", None, None),
            P("expert", None, None),
        ),
        out_specs=(P(("dp", "expert"), None), P("expert", "dp", None), P("expert", "dp", None)),
        check_vma=False,
    )
```

profile of v0, /device:TPU:2, one launch (start us, length us, event | category | flops | bytes accessed | tf_op | source)
XLA Modules:
  0.0 295.7 jit_solution(2285066846096430929)
XLA Ops:
  7.2 0.0 copy-start
  7.2 0.0 all-gather.5.cloned.1.call-start
  7.2 0.7 all-gather.5.cloned.1.call-update
  7.9 0.0 all-gather.3.cloned.1.call-start
  8.0 0.7 all-gather.3.cloned.1.call-update
  8.7 0.0 reduce-scatter.4.cloned.1.call-start
  8.7 0.7 convert_element_type.48
  9.4 1.3 dynamic-slice
  11.3 0.2 dynamic-update-slice
  11.6 31.3 %all-reduce.2 = bf16[2560]{0:T(1024)(128)(2,1)S(1)} all-reduce(bf16[2560]{0:T(1024)(128)(2,1)S(1)} %dynamic-update-slice), channel_id=1, replica_groups=mesh['dp'=16,'expert'=16] {'expert'}, use_global_device_ids=true, to_apply=%add.2 | all-reduce | flops 2560 | bytes 10240
  42.9 0.1 reshape.70
  42.9 0.6 reduce-window.16
  43.5 0.2 slice_reduce_fusion
  43.8 0.1 copy_bitcast_fusion
  43.9 35.2 %all-gather.5.cloned.1.call-done = bf16[2560,2048]{1,0:T(8,128)(2,1)} async-done(((bf16[160,2048]{1,0:T(8,128)(2,1)}), bf16[2560,2048]{1,0:T(8,128)(2,1)}) %all-gather.5.cloned.1.call-update) | async-done | bytes 10485776 | tf_op jit(solution)/shard_map/all_gather | solution.py:27
  79.1 6.8 %convolution_convert_fusion.2 = bf16[16,30,2048]{2,1,0:T(8,128)(2,1)} fusion(bf16[16,160,2048]{2,1,0:T(8,128)(2,1)} %bitcast.48, s32[16,160]{1,0:T(8,128)S(1)} %slice_add_fusion, pred[16,160]{1,0:T(8,128)(4,1)S(1)} %broadcast_compare_fusion), kind=kOutput, calls=%fused_computation.9 | convolution fusion | flops 315709440 | bytes 12464640 | tf_op jit(solution)/shard_map/jct,jtd->jcd/dot_general | solution.py:39
  85.9 2.8 convert_element_type.55
  88.7 56.5 %all-gather.3.cloned.1.call-done = bf16[2560,2048]{1,0:T(8,128)(2,1)} async-done(((bf16[160,2048]{1,0:T(8,128)(2,1)}), bf16[2560,2048]{1,0:T(8,128)(2,1)}) %all-gather.3.cloned.1.call-update) | async-done | bytes 10485776 | tf_op jit(solution)/shard_map/all_gather | solution.py:28
  145.2 6.8 %convolution_convert_fusion.3 = bf16[16,30,2048]{2,1,0:T(8,128)(2,1)} fusion(bf16[16,160,2048]{2,1,0:T(8,128)(2,1)} %bitcast.49, s32[16,160]{1,0:T(8,128)S(1)} %slice_add_fusion, pred[16,160]{1,0:T(8,128)(4,1)S(1)} %broadcast_compare_fusion), kind=kOutput, calls=%fused_computation.10 | convolution fusion | flops 315709440 | bytes 12464640 | tf_op jit(solution)/shard_map/jct,jtd->jcd/dot_general | solution.py:46
  151.9 2.8 convert_element_type.53
  154.7 0.0 copy-start.3
  154.7 6.0 %fusion.2 = f32[480,1536]{1,0:T(8,128)S(1)} fusion(bf16[480,2048]{1,0:T(8,128)(2,1)} %convert_element_type.55, bf16[1,2048,1536]{2,1,0:T(8,128)(2,1)} %param.8), kind=kOutput, calls=%fused_computation.4 | convolution fusion | flops 3019898880 | bytes 11206656 | tf_op jit(solution)/shard_map/dot_general | solution.py:55
  160.8 0.0 copy-done.3
  160.8 1.9 convolution_convert_fusion.1
  162.7 0.0 copy-done
  162.7 0.0 copy-start.2
  162.7 2.0 multiply_convert_fusion.2
  164.7 0.0 copy-start.5
  164.7 0.0 copy-start.7
  164.7 0.0 copy-done.2
  164.8 3.8 %convolution_convert_fusion = bf16[2048,1536]{0,1:T(8,128)(2,1)S(1)} fusion(bf16[480,2048]{1,0:T(8,128)(2,1)S(1)} %copy-done.2, bf16[480,768]{1,0:T(8,128)(2,1)S(1)} %get-tuple-element.13, bf16[480,768]{1,0:T(8,128)(2,1)S(1)} %get-tuple-element.12), kind=kOutput, calls=%fused_computation.1 | convolution fusion | flops 3025993728 | bytes 9732096 | tf_op jit(solution)/shard_map/dot_general | solution.py:72
  168.6 0.0 copy-done.5
  168.6 0.0 copy-done.7
  168.6 11.5 %pad_maximum_fusion = bf16[2048,2304]{0,1:T(8,128)(2,1)} fusion(bf16[2048,768]{0,1:T(8,128)(2,1)S(1)} %convolution_convert_fusion.1, bf16[2048,1536]{0,1:T(8,128)(2,1)S(1)} %convolution_convert_fusion), kind=kLoop, calls=%fused_computation | loop fusion | flops 18874368 | bytes 18874368 | tf_op jit(solution)/shard_map/concatenate | solution.py:79
  180.1 12.2 %copy.22 = bf16[2048,2304]{1,0:T(8,128)(2,1)} copy(bf16[2048,2304]{0,1:T(8,128)(2,1)} %pad_maximum_fusion) | data formatting | bytes 18874368
  192.3 0.0 copy-start.6
  192.3 0.0 reduce-scatter.4.cloned.1.call-update
  192.3 1.1 copy-done.6
  193.4 6.3 %fusion.6 = bf16[480,2048]{1,0:T(8,128)(2,1)S(1)} fusion(bf16[1,2048,1536]{2,1,0:T(8,128)(2,1)} %param.8, bf16[480,768]{1,0:T(8,128)(2,1)} %copy-done.7, bf16[480,768]{1,0:T(8,128)(2,1)S(1)} %copy-done.6), kind=kOutput, calls=%fused_computation.11 | convolution fusion | flops 3023831040 | bytes 9732096 | tf_op jit(solution)/shard_map/dot_general | solution.py:65
  199.7 1.6 all_to_all.8
  201.3 0.0 copy-start.4
  201.3 4.5 %all-to-all-start = ((bf16[16,30,2048]{2,1,0:T(8,128)(2,1)}), bf16[16,30,2048]{2,1,0:T(8,128)(2,1)S(1)}, u32[]{:S(2)}, u32[]{:S(2)}) async-start(bf16[16,30,2048]{2,1,0:T(8,128)(2,1)} %all_to_all.8), calls=%async_computation | async-start | bytes 4194304 | tf_op jit(solution)/shard_map/all_to_all | solution.py:68
  205.8 0.0 copy-done.4
  205.8 0.6 reduce-window.14
  206.4 0.2 slice_reduce_fusion.1
  206.6 0.1 bitcast_bitcast_fusion
  206.8 48.2 %all-to-all-done = bf16[16,30,2048]{2,1,0:T(8,128)(2,1)S(1)} async-done(((bf16[16,30,2048]{2,1,0:T(8,128)(2,1)}), bf16[16,30,2048]{2,1,0:T(8,128)(2,1)S(1)}, u32[]{:S(2)}, u32[]{:S(2)}) %all-to-all-start) | async-done | bytes 1966112 | tf_op jit(solution)/shard_map/all_to_all | solution.py:68
  255.0 1.5 all_to_all.10
  256.5 0.0 copy-start.1
  256.5 3.1 %convolution_convert_fusion.4 = bf16[160,2048]{1,0:T(8,128)(2,1)} fusion(bf16[480,2048]{1,0:T(8,128)(2,1)} %all_to_all.10, s32[160]{0:T(256)S(1)} %multiply_add_fusion), kind=kOutput, calls=%fused_computation.12 | convolution fusion | flops 314977280 | bytes 2622080 | tf_op jit(solution)/shard_map/dot_general | solution.py:69
  259.6 23.7 %reduce-scatter.4.cloned.1.call-done = bf16[128,2304]{1,0:T(8,128)(2,1)} async-done(((bf16[2048,2304]{1,0:T(8,128)(2,1)}), bf16[128,2304]{1,0:T(8,128)(2,1)}) %reduce-scatter.4.cloned.1.call-update) | async-done | bytes 589840
  283.3 1.8 slice.48
  285.1 1.2 copy.24
  286.3 0.9 copy.20
  287.2 0.9 slice.49
  288.2 0.2 copy.25
  288.3 0.8 copy.21
  289.2 0.0 copy-done.1
  (13 shorter events, 0.2 us)
Async XLA Ops:
  7.2 155.5 %copy-start = (bf16[1,2048,768]{2,1,0:T(8,128)(2,1)S(1)}, bf16[1,2048,768]{2,1,0:T(8,128)(2,1)}, u32[]{:S(2)}) copy-start(bf16[1,2048,768]{2,1,0:T(8,128)(2,1)} %param.9) | copy-start | bytes 9437188
  7.2 71.9 %all-gather.5.cloned.1.call-start = ((), (), s32[]{:S(2)}) async-start(), calls=%async_computation.3 | async-start | bytes 11141120 | tf_op jit(solution)/shard_map/all_gather | solution.py:27
  7.9 137.2 %all-gather.3.cloned.1.call-start = ((), (), s32[]{:S(2)}) async-start(), calls=%async_computation.2 | async-start | bytes 11141120 | tf_op jit(solution)/shard_map/all_gather | solution.py:28
  8.7 274.6 %reduce-scatter.4.cloned.1.call-start = ((), (), s32[]{:S(2)}) async-start(), calls=%async_computation.4 | async-start | bytes 10027008
  154.7 6.1 %copy-start.3 = (bf16[480,2048]{1,0:T(8,128)(2,1)S(1)}, bf16[480,2048]{1,0:T(8,128)(2,1)}, u32[]{:S(2)}) copy-start(bf16[480,2048]{1,0:T(8,128)(2,1)} %convert_element_type.53) | copy-start | bytes 5898244
  162.7 2.0 copy-start.2
  164.7 3.9 %copy-start.5 = (bf16[480,768]{1,0:T(8,128)(2,1)}, bf16[480,768]{1,0:T(8,128)(2,1)S(1)}, u32[]{:S(2)}) copy-start(bf16[480,768]{1,0:T(8,128)(2,1)S(1)} %get-tuple-element.12) | copy-start | bytes 2211844
  164.7 3.9 %copy-start.7 = (bf16[480,768]{1,0:T(8,128)(2,1)}, bf16[480,768]{1,0:T(8,128)(2,1)S(1)}, u32[]{:S(2)}) copy-start(bf16[480,768]{1,0:T(8,128)(2,1)S(1)} %get-tuple-element.13) | copy-start | bytes 2211844
  192.3 1.1 copy-start.6
  201.3 4.5 %copy-start.4 = (s32[160,1]{0,1:T(1,128)S(1)}, s32[160,1]{0,1:T(1,128)}, u32[]{:S(2)}) copy-start(s32[160,1]{0,1:T(1,128)} %param.7) | copy-start | bytes 1924
  201.3 53.7 %all-to-all-start = ((bf16[16,30,2048]{2,1,0:T(8,128)(2,1)}), bf16[16,30,2048]{2,1,0:T(8,128)(2,1)S(1)}, u32[]{:S(2)}, u32[]{:S(2)}) async-start(bf16[16,30,2048]{2,1,0:T(8,128)(2,1)} %all_to_all.8), calls=%async_computation | async-start | bytes 4194304 | tf_op jit(solution)/shard_map/all_to_all | solution.py:68
  256.5 32.7 %copy-start.1 = (bf16[1,2048,768]{2,1,0:T(8,128)(2,1)S(1)}, bf16[1,2048,768]{2,1,0:T(8,128)(2,1)}, u32[]{:S(2)}) copy-start(bf16[1,2048,768]{2,1,0:T(8,128)(2,1)} %param.9) | copy-start | bytes 9437188
Sparse Core Ops, SparseCore 0:
  9.8 69.1 all-gather.4
  80.9 64.2 all-gather.2
  192.4 90.8 reduce-scatter.3
where the time goes:
time: 296 us
  waiting for transfers between devices  165 us (56%)
  matrix products  36.7 us (12%)
  blocking collectives  31.3 us (11%)
  local copies, waits for them, and re-layouts  29.8 us (10%)
  between operations  14.6 us (5%)
  other arithmetic  13.7 us (5%)
  starting transfers between devices  4.62 us (2%)
    all_gather x1, waiting for transfers between devices, local(): lax.all_gather(out_grads, 'expert', axis=0, tiled=True)  56.5 us
    all_to_all x1, waiting for transfers between devices, local(): lax.all_to_all(drows, 'expert', split_axis=0, concat_axis=0, tiled=True)  48.2 us
    all_gather x1, waiting for transfers between devices, local(): lax.all_gather(tokens, 'expert', axis=0, tiled=True)  35.2 us
    unnamed x1, blocking collectives  31.3 us
    unnamed x4, waiting for transfers between devices  25.1 us
    unnamed x24, local copies, waits for them, and re-layouts  17.9 us
    concatenate x1, other arithmetic, local(): jnp.concatenate([first, second], axis=1).astype(jnp.bfloat16)  11.5 us
    dot_general x1, matrix products, local(): jnp.einsum('jct,jtd->jcd', select, all_x.reshape(num_experts, tok_rows, w...  6.8 us
  transfers between devices with their start and end apart: 4, of which 4 were waited for; matrix products, arithmetic and copies ran while one was open for 8% of the time, Pallas kernels for 0%

commit v1 on v0

v1 whole, which is shorter than its diff:
```python
import jax
import jax.numpy as jnp
from jax import lax
from jax.sharding import PartitionSpec as P

SLOTS = 32


def slot_table(routed, num_experts):
    rows = routed.shape[0]
    places = jnp.arange(rows, dtype=jnp.int32)
    same = (routed[:, None] == routed[None, :]) & (places[:, None] < places[None, :])
    slots = jnp.sum(same.astype(jnp.int32), axis=0)
    target = routed * SLOTS + slots
    spots = jnp.arange(num_experts * SLOTS, dtype=jnp.int32)
    return (spots[:, None] == target[None, :]).astype(jnp.bfloat16)


def local(tokens, out_grads, expert_ids, w_gate_up, w_down_t):
    num_experts = lax.axis_size("expert")
    width = tokens.shape[1]
    ff = w_down_t.shape[2]
    dispatch = slot_table(expert_ids[:, 0], num_experts)

    def send(rows):
        slots = jnp.dot(dispatch, rows, preferred_element_type=jnp.float32).astype(jnp.bfloat16)
        slots = slots.reshape(num_experts, SLOTS, width)
        got = lax.all_to_all(slots, "expert", split_axis=0, concat_axis=0, tiled=True)
        return got.reshape(num_experts * SLOTS, width)

    rows_x = send(tokens)
    rows_dy = send(out_grads)
    w_in = w_gate_up[0]
    w_out = w_down_t[0]
    gate_up = jnp.dot(rows_x, w_in, preferred_element_type=jnp.float32)
    gate = gate_up[:, :ff]
    upper = gate_up[:, ff:]
    sig = jax.nn.sigmoid(gate)
    silu = gate * sig
    hidden = (silu * upper).astype(jnp.bfloat16)
    dhidden = jnp.dot(rows_dy, w_out, preferred_element_type=jnp.float32)
    dgate = dhidden * upper * sig * (1.0 + gate * (1.0 - sig))
    dupper = dhidden * silu
    dgate_up = jnp.concatenate([dgate, dupper], axis=1).astype(jnp.bfloat16)
    drows = lax.dot_general(
        dgate_up, w_in, (((1,), (1,)), ((), ())), preferred_element_type=jnp.float32
    ).astype(jnp.bfloat16)
    returned = lax.all_to_all(
        drows.reshape(num_experts, SLOTS, width), "expert", split_axis=0, concat_axis=0, tiled=True
    ).reshape(num_experts * SLOTS, width)
    token_grads = lax.dot_general(
        dispatch, returned, (((0,), (0,)), ((), ())), preferred_element_type=jnp.float32
    ).astype(jnp.bfloat16)
    first = lax.dot_general(
        rows_x, dgate_up, (((0,), (0,)), ((), ())), preferred_element_type=jnp.float32
    ).astype(jnp.bfloat16)
    second = lax.dot_general(
        rows_dy, hidden, (((0,), (0,)), ((), ())), preferred_element_type=jnp.float32
    ).astype(jnp.bfloat16)
    grad_gate_up = lax.psum_scatter(first, "dp", scatter_dimension=0, tiled=True)[None]
    grad_down_t = lax.psum_scatter(second, "dp", scatter_dimension=0, tiled=True)[None]
    return (token_grads, grad_gate_up, grad_down_t)


def solution(mesh):
    return jax.shard_map(
        local,
        mesh=mesh,
        in_specs=(
            P(("dp", "expert"), None),
            P(("dp", "expert"), None),
            P(("dp", "expert"), None),
            P("expert", None, None),
            P("expert", None, None),
        ),
        out_specs=(P(("dp", "expert"), None), P("expert", "dp", None), P("expert", "dp", None)),
        check_vma=False,
    )
```

time: 296 us -> 307 us (1.037)
  local copies, waits for them, and re-layouts: 29.8 us -> 1.17 us
  blocking collectives: 31.3 us -> 54.3 us
  waiting for transfers between devices: 165 us -> 181 us
  other arithmetic: 13.7 us -> 1.65 us
  starting transfers between devices: 4.62 us -> 13.7 us
  matrix products: 36.7 us -> 40.8 us
    reduce_scatter x0 -> x2, waiting for transfers between devices: none -> 94.1 us  [the longest x1 90.1 us: local(): lax.psum_scatter(first, 'dp', scatter_dimension=0, tiled=True)[None]]
    all_gather x2 -> x0, waiting for transfers between devices: 91.7 us -> none  [the longest x1 56.5 us: local(): lax.all_gather(out_grads, 'expert', axis=0, tiled=True)]
    all_to_all x0 -> x1, blocking collectives: none -> 54.3 us  [local(): lax.all_to_all(drows.reshape(num_experts, SLOTS, width), 'expert', split_...]
    all_to_all x1 -> x2, waiting for transfers between devices: 48.2 us -> 86.8 us  [send(): lax.all_to_all(slots, 'expert', split_axis=0, concat_axis=0, tiled=True)]
    unnamed x1 -> x0, blocking collectives: 31.3 us -> none
    unnamed x4 -> x2, waiting for transfers between devices: 25.1 us -> 0.03 us
    unnamed x24 -> x6, local copies, waits for them, and re-layouts: 17.9 us -> 1.17 us
    concatenate x1 -> x0, other arithmetic: 11.5 us -> none  [local(): jnp.concatenate([first, second], axis=1).astype(jnp.bfloat16)]
  transfers between devices with their start and end apart: 4 -> 4, of which waited for: 4 -> 4; matrix products, arithmetic and copies ran while one was open for 8% -> 10% of each run, Pallas kernels for 0% -> 0%
where the time goes in v1:
time: 307 us
  waiting for transfers between devices  181 us (59%)
  blocking collectives  54.3 us (18%)
  matrix products  40.8 us (13%)
  between operations  14.1 us (5%)
  starting transfers between devices  13.7 us (4%)
    reduce_scatter x1, waiting for transfers between devices, local(): lax.psum_scatter(first, 'dp', scatter_dimension=0, tiled=True)[None]  90.1 us
    all_to_all x2, waiting for transfers between devices, send(): lax.all_to_all(slots, 'expert', split_axis=0, concat_axis=0, tiled=True)  86.8 us
    all_to_all x1, blocking collectives, local(): lax.all_to_all(drows.reshape(num_experts, SLOTS, width), 'expert', split_...  54.3 us
    all_to_all x2, starting transfers between devices, send(): lax.all_to_all(slots, 'expert', split_axis=0, concat_axis=0, tiled=True)  13.4 us
    dot_general x1, matrix products, local(): gate_up = jnp.dot(rows_x, w_in, preferred_element_type=jnp.float32)  8.49 us
    dot_general x1, matrix products, local(): lax.dot_general(rows_x, dgate_up, (((0,), (0,)), ((), ())), preferred_ele...  7.1 us
    dot_general x1, matrix products, local(): lax.dot_general(dgate_up, w_in, (((1,), (1,)), ((), ())), preferred_eleme...  6.74 us
    dot_general x2, matrix products, send(): jnp.dot(dispatch, rows, preferred_element_type=jnp.float32)  6.33 us
  transfers between devices with their start and end apart: 4, of which 4 were waited for; matrix products, arithmetic and copies ran while one was open for 10% of the time, Pallas kernels for 0%

profile of v1, /device:TPU:2, one launch (start us, length us, event | category | flops | bytes accessed | tf_op | source)
XLA Modules:
  0.0 306.6 jit_solution(7016371018986152856)
XLA Ops:
  7.2 0.0 copy-start
  7.2 0.9 convert_reduce_fusion
  8.1 0.7 multiply_add_fusion
  8.8 3.2 %convolution_convert_fusion.2 = bf16[512,2048]{1,0:T(8,128)(2,1)} fusion(bf16[160,2048]{1,0:T(8,128)(2,1)} %param.5, s32[160]{0:T(256)S(1)} %multiply_add_fusion), kind=kOutput, calls=%fused_computation.8 | convolution fusion | flops 336674816 | bytes 2753152 | tf_op jit(solution)/shard_map/dot_general | solution.py:26
  12.0 8.6 %all-to-all-start.1 = ((bf16[16,32,2048]{2,1,0:T(8,128)(2,1)}), bf16[16,32,2048]{2,1,0:T(8,128)(2,1)}, u32[]{:S(2)}, u32[]{:S(2)}) async-start(bf16[16,32,2048]{2,1,0:T(8,128)(2,1)} %bitcast.29), calls=%async_computation.1 | async-start | bytes 4194304 | tf_op jit(solution)/shard_map/all_to_all | solution.py:28
  20.6 3.2 %convolution_convert_fusion.3 = bf16[512,2048]{1,0:T(8,128)(2,1)} fusion(bf16[160,2048]{1,0:T(8,128)(2,1)} %param.6, s32[160]{0:T(256)S(1)} %multiply_add_fusion), kind=kOutput, calls=%fused_computation.9 | convolution fusion | flops 336674816 | bytes 2753152 | tf_op jit(solution)/shard_map/dot_general | solution.py:26
  23.8 46.1 %all-to-all-done.1 = bf16[16,32,2048]{2,1,0:T(8,128)(2,1)} async-done(((bf16[16,32,2048]{2,1,0:T(8,128)(2,1)}), bf16[16,32,2048]{2,1,0:T(8,128)(2,1)}, u32[]{:S(2)}, u32[]{:S(2)}) %all-to-all-start.1) | async-done | bytes 2097184 | tf_op jit(solution)/shard_map/all_to_all | solution.py:28
  69.9 4.8 %all-to-all-start = ((bf16[16,32,2048]{2,1,0:T(8,128)(2,1)}), bf16[16,32,2048]{2,1,0:T(8,128)(2,1)}, u32[]{:S(2)}, u32[]{:S(2)}) async-start(bf16[16,32,2048]{2,1,0:T(8,128)(2,1)} %bitcast.28), calls=%async_computation | async-start | bytes 4194304 | tf_op jit(solution)/shard_map/all_to_all | solution.py:28
  74.7 0.0 reduce-scatter.5.cloned.1.call-start
  74.7 8.5 %fusion.2 = f32[512,1536]{1,0:T(8,128)} fusion(bf16[512,2048]{1,0:T(8,128)(2,1)} %bitcast.5, bf16[1,2048,1536]{2,1,0:T(8,128)(2,1)} %param.8), kind=kOutput, calls=%fused_computation.3 | convolution fusion | flops 3221225472 | bytes 11534336 | tf_op jit(solution)/shard_map/dot_general | solution.py:35
  83.2 40.7 %all-to-all-done = bf16[16,32,2048]{2,1,0:T(8,128)(2,1)} async-done(((bf16[16,32,2048]{2,1,0:T(8,128)(2,1)}), bf16[16,32,2048]{2,1,0:T(8,128)(2,1)}, u32[]{:S(2)}, u32[]{:S(2)}) %all-to-all-start) | async-done | bytes 2097184 | tf_op jit(solution)/shard_map/all_to_all | solution.py:28
  123.9 6.1 %convolution_convert_fusion.1 = bf16[2048,768]{1,0:T(8,128)(2,1)} fusion(bf16[512,2048]{1,0:T(8,128)(2,1)} %bitcast.2, f32[512,1536]{1,0:T(8,128)} %fusion.2), kind=kOutput, calls=%fused_computation.5 | convolution fusion | flops 1614544896 | bytes 8388608 | tf_op jit(solution)/shard_map/dot_general | solution.py:57
  130.0 0.0 reduce-scatter.5.cloned.1.call-update
  130.1 0.2 reduce-scatter.3.cloned.1.call-start
  130.3 0.0 copy-done
  130.3 4.6 %multiply_convert_fusion.2 = (bf16[512,768]{1,0:T(8,128)(2,1)S(1)}, bf16[512,768]{1,0:T(8,128)(2,1)S(1)}) fusion(f32[512,1536]{1,0:T(8,128)} %fusion.2, bf16[512,2048]{1,0:T(8,128)(2,1)} %bitcast.2, bf16[1,2048,768]{2,1,0:T(8,128)(2,1)S(1)} %copy-done), kind=kOutput, calls=%fused_computation.15 | convolution fusion | flops 1615724544 | bytes 9961472 | tf_op jit(solution)/shard_map/dot_general | solution.py:41
  134.9 0.0 copy-start.1
  134.9 0.0 copy-start.2
  135.0 0.9 copy-done.1
  135.9 0.3 copy-done.2
  136.1 7.1 %convolution_convert_fusion = bf16[2048,1536]{1,0:T(8,128)(2,1)} fusion(bf16[512,2048]{1,0:T(8,128)(2,1)} %bitcast.5, bf16[512,768]{1,0:T(8,128)(2,1)S(1)} %get-tuple-element.4, bf16[512,768]{1,0:T(8,128)(2,1)S(1)} %get-tuple-element.3), kind=kOutput, calls=%fused_computation | convolution fusion | flops 3227516928 | bytes 9961472 | tf_op jit(solution)/shard_map/dot_general | solution.py:54
  143.2 0.0 reduce-scatter.3.cloned.1.call-update
  143.2 6.7 %fusion.6 = bf16[512,2048]{1,0:T(8,128)(2,1)S(1)} fusion(bf16[1,2048,1536]{2,1,0:T(8,128)(2,1)} %param.8, bf16[512,768]{1,0:T(8,128)(2,1)} %copy-done.2, bf16[512,768]{1,0:T(8,128)(2,1)} %copy-done.1), kind=kOutput, calls=%fused_computation.10 | convolution fusion | flops 3225419776 | bytes 9961472 | tf_op jit(solution)/shard_map/dot_general | solution.py:45
  150.0 54.3 %all_to_all.15 = bf16[16,32,2048]{2,1,0:T(8,128)(2,1)S(1)} all-to-all(bf16[16,32,2048]{2,1,0:T(8,128)(2,1)S(1)} %bitcast.31), channel_id=1, replica_groups=mesh['dp'=16,'expert'=16] {'expert'}, dimensions={0} | all-to-all | bytes 4194304 | tf_op jit(solution)/shard_map/all_to_all | solution.py:48
  204.3 1.4 convolution_convert_fusion.4
  205.7 4.0 %reduce-scatter.5.cloned.1.call-done = bf16[128,768]{1,0:T(8,128)(2,1)} async-done(((bf16[2048,768]{1,0:T(8,128)(2,1)}), bf16[128,768]{1,0:T(8,128)(2,1)}) %reduce-scatter.5.cloned.1.call-update) | async-done | bytes 196624 | tf_op jit(solution)/shard_map/reduce_scatter | solution.py:61
  209.7 90.1 %reduce-scatter.3.cloned.1.call-done = bf16[128,1536]{1,0:T(8,128)(2,1)} async-done(((bf16[2048,1536]{1,0:T(8,128)(2,1)}), bf16[128,1536]{1,0:T(8,128)(2,1)}) %reduce-scatter.3.cloned.1.call-update) | async-done | bytes 393232 | tf_op jit(solution)/shard_map/reduce_scatter | solution.py:60
Async XLA Ops:
  7.2 123.1 %copy-start = (bf16[1,2048,768]{2,1,0:T(8,128)(2,1)S(1)}, bf16[1,2048,768]{2,1,0:T(8,128)(2,1)}, u32[]{:S(2)}) copy-start(bf16[1,2048,768]{2,1,0:T(8,128)(2,1)} %param.9) | copy-start | bytes 9437188
  12.0 57.9 %all-to-all-start.1 = ((bf16[16,32,2048]{2,1,0:T(8,128)(2,1)}), bf16[16,32,2048]{2,1,0:T(8,128)(2,1)}, u32[]{:S(2)}, u32[]{:S(2)}) async-start(bf16[16,32,2048]{2,1,0:T(8,128)(2,1)} %bitcast.29), calls=%async_computation.1 | async-start | bytes 4194304 | tf_op jit(solution)/shard_map/all_to_all | solution.py:28
  69.9 54.0 %all-to-all-start = ((bf16[16,32,2048]{2,1,0:T(8,128)(2,1)}), bf16[16,32,2048]{2,1,0:T(8,128)(2,1)}, u32[]{:S(2)}, u32[]{:S(2)}) async-start(bf16[16,32,2048]{2,1,0:T(8,128)(2,1)} %bitcast.28), calls=%async_computation | async-start | bytes 4194304 | tf_op jit(solution)/shard_map/all_to_all | solution.py:28
  74.7 135.0 %reduce-scatter.5.cloned.1.call-start = ((), (), s32[]{:S(2)}) async-start(), calls=%async_computation.6 | async-start | bytes 3342336 | tf_op jit(solution)/shard_map/reduce_scatter | solution.py:61
  130.1 169.7 %reduce-scatter.3.cloned.1.call-start = ((), (), s32[]{:S(2)}) async-start(), calls=%async_computation.5 | async-start | bytes 6684672 | tf_op jit(solution)/shard_map/reduce_scatter | solution.py:60
  134.9 0.9 copy-start.1
  134.9 1.2 copy-start.2
Sparse Core Ops, SparseCore 0:
  130.2 79.4 reduce-scatter.4
  214.0 85.7 reduce-scatter.2

commit v2 on v1

--- a/solution.py
+++ b/solution.py
@@ -14,6 +14,57 @@
     target = routed * SLOTS + slots
     spots = jnp.arange(num_experts * SLOTS, dtype=jnp.int32)
     return (spots[:, None] == target[None, :]).astype(jnp.bfloat16)
+
+
+def pair_perm(axis, odd):
+    def mate(i):
+        return (i ^ 1) if not odd else (3 - i)
+
+    return [
+        (x * 4 + y, mate(x) * 4 + y if axis == 0 else x * 4 + mate(y))
+        for x in range(4)
+        for y in range(4)
+    ]
+
+
+def scatter_sum(partial):
+    me = lax.axis_index("dp")
+    at = (me // 4, me % 4)
+    cols = partial.shape[1]
+    rows = partial.shape[0] // 64
+    view = partial.reshape(4, 4, 4, rows, cols)
+
+    def half(block, axis, first_odd, step):
+        i = at[axis]
+        if step == 0:
+            if first_odd:
+                low, high = lax.slice_in_dim(block, 0, 2, 1, axis), lax.slice_in_dim(block, 2, 4, 1, axis)
+                mine_low = i < 2
+            else:
+                low, high = lax.slice_in_dim(block, 0, 4, 3, axis), lax.slice_in_dim(block, 1, 3, 1, axis)
+                mine_low = (i == 0) | (i == 3)
+        else:
+            low, high = lax.slice_in_dim(block, 0, 1, 1, axis), lax.slice_in_dim(block, 1, 2, 1, axis)
+            mine_low = (i % 2 == 0) if first_odd else (i < 2)
+        return jnp.where(mine_low, high, low), jnp.where(mine_low, low, high)
+
+    plans = (
+        ((0, False), (0, True), (1, False), (1, True)),
+        ((0, True), (0, False), (1, True), (1, False)),
+        ((1, False), (1, True), (0, False), (0, True)),
+        ((1, True), (1, False), (0, True), (0, False)),
+    )
+    blocks = [view[:, :, f] for f in range(4)]
+    for step in range(4):
+        out = []
+        for block, plan in zip(blocks, plans):
+            axis, odd = plan[step]
+            first_odd = plan[step - step % 2][1]
+            give, keep = half(block, axis, first_odd, step % 2)
+            got = lax.ppermute(give, "dp", pair_perm(axis, odd))
+            out.append((keep.astype(jnp.float32) + got.astype(jnp.float32)).astype(jnp.bfloat16))
+        blocks = out
+    return jnp.concatenate([b.reshape(rows, cols) for b in blocks], axis=0)
 
 
 def local(tokens, out_grads, expert_ids, w_gate_up, w_down_t):
@@ -57,9 +108,8 @@
     second = lax.dot_general(
         rows_dy, hidden, (((0,), (0,)), ((), ())), preferred_element_type=jnp.float32
     ).astype(jnp.bfloat16)
-    grad_gate_up = lax.psum_scatter(first, "dp", scatter_dimension=0, tiled=True)[None]
-    grad_down_t = lax.psum_scatter(second, "dp", scatter_dimension=0, tiled=True)[None]
-    return (token_grads, grad_gate_up, grad_down_t)
+    summed = scatter_sum(jnp.concatenate([first, second], axis=1))
+    return (token_grads, summed[None, :, : 2 * ff], summed[None, :, 2 * ff :])
 
 
 def solution(mesh):

time: 307 us -> 242 us (0.79)
  blocking collectives: 54.3 us -> 0 us
  waiting for transfers between devices: 181 us -> 127 us
  starting transfers between devices: 13.7 us -> 42.8 us
  local copies, waits for them, and re-layouts: 1.17 us -> 17.3 us
  between operations: 14.1 us -> 0.98 us
  other arithmetic: 1.65 us -> 13.8 us
    reduce_scatter x2 -> x0, waiting for transfers between devices: 94.1 us -> none  [the longest x1 90.1 us: local(): lax.psum_scatter(first, 'dp', scatter_dimension=0, tiled=True)[None]]
    all_to_all x1 -> x0, blocking collectives: 54.3 us -> none  [local(): lax.all_to_all(drows.reshape(num_experts, SLOTS, width), 'expert', split_...]
    ppermute x0 -> x16, waiting for transfers between devices: none -> 40.2 us  [scatter_sum(): got = lax.ppermute(give, 'dp', pair_perm(axis, odd))]
    ppermute x0 -> x16, starting transfers between devices: none -> 24.3 us  [scatter_sum(): got = lax.ppermute(give, 'dp', pair_perm(axis, odd))]
    concatenate x0 -> x1, local copies, waits for them, and re-layouts: none -> 12.7 us  [local(): summed = scatter_sum(jnp.concatenate([first, second], axis=1))]
    concatenate x0 -> x2, other arithmetic: none -> 7 us  [the longest x1 6.96 us: local(): summed = scatter_sum(jnp.concatenate([first, second], axis=1))]
    all_to_all x0 -> x1, starting transfers between devices: none -> 5.07 us  [local(): lax.all_to_all(drows.reshape(num_experts, SLOTS, width), 'expert', split_...]
    squeeze x0 -> x1, local copies, waits for them, and re-layouts: none -> 3.71 us  [scatter_sum(): blocks = [view[:, :, f] for f in range(4)]]
  transfers between devices with their start and end apart: 4 -> 19, of which waited for: 4 -> 12; matrix products, arithmetic and copies ran while one was open for 10% -> 17% of each run, Pallas kernels for 0% -> 0%
where the time goes in v2:
time: 242 us
  waiting for transfers between devices  127 us (52%)
  starting transfers between devices  42.8 us (18%)
  matrix products  39.8 us (16%)
  local copies, waits for them, and re-layouts  17.3 us (7%)
  other arithmetic  13.8 us (6%)
    all_to_all x2, waiting for transfers between devices, send(): lax.all_to_all(slots, 'expert', split_axis=0, concat_axis=0, tiled=True)  86.7 us
    ppermute x16, waiting for transfers between devices, scatter_sum(): got = lax.ppermute(give, 'dp', pair_perm(axis, odd))  40.2 us
    ppermute x16, starting transfers between devices, scatter_sum(): got = lax.ppermute(give, 'dp', pair_perm(axis, odd))  24.3 us
    all_to_all x2, starting transfers between devices, send(): lax.all_to_all(slots, 'expert', split_axis=0, concat_axis=0, tiled=True)  13.4 us
    concatenate x1, local copies, waits for them, and re-layouts, local(): summed = scatter_sum(jnp.concatenate([first, second], axis=1))  12.7 us
    dot_general x1, matrix products, local(): gate_up = jnp.dot(rows_x, w_in, preferred_element_type=jnp.float32)  8.52 us
    dot_general x1, matrix products, local(): lax.dot_general(rows_x, dgate_up, (((0,), (0,)), ((), ())), preferred_ele...  6.97 us
    concatenate x1, other arithmetic, local(): summed = scatter_sum(jnp.concatenate([first, second], axis=1))  6.96 us
  transfers between devices with their start and end apart: 19, of which 12 were waited for; matrix products, arithmetic and copies ran while one was open for 17% of the time, Pallas kernels for 0%

profile of v2, /device:TPU:2, one launch (start us, length us, event | category | flops | bytes accessed | tf_op | source)
XLA Modules:
  0.0 241.6 jit_solution(8573421623701064685)
XLA Ops:
  0.6 0.9 convert_reduce_fusion
  1.6 0.7 multiply_add_fusion
  2.3 3.1 %convolution_convert_fusion.2 = bf16[512,2048]{1,0:T(8,128)(2,1)} fusion(bf16[160,2048]{1,0:T(8,128)(2,1)} %param.5, s32[160]{0:T(256)S(1)} %multiply_add_fusion), kind=kOutput, calls=%fused_computation.9 | convolution fusion | flops 336674816 | bytes 2753152 | tf_op jit(solution)/shard_map/dot_general | solution.py:77
  5.4 8.6 %all-to-all-start.1 = ((bf16[16,32,2048]{2,1,0:T(8,128)(2,1)}), bf16[16,32,2048]{2,1,0:T(8,128)(2,1)}, u32[]{:S(2)}, u32[]{:S(2)}) async-start(bf16[16,32,2048]{2,1,0:T(8,128)(2,1)} %bitcast.79), calls=%async_computation.1 | async-start | bytes 4194304 | tf_op jit(solution)/shard_map/all_to_all | solution.py:79
  14.0 3.1 %convolution_convert_fusion.3 = bf16[512,2048]{1,0:T(8,128)(2,1)} fusion(bf16[160,2048]{1,0:T(8,128)(2,1)} %param.6, s32[160]{0:T(256)S(1)} %multiply_add_fusion), kind=kOutput, calls=%fused_computation.10 | convolution fusion | flops 336674816 | bytes 2753152 | tf_op jit(solution)/shard_map/dot_general | solution.py:77
  17.2 46.1 %all-to-all-done.1 = bf16[16,32,2048]{2,1,0:T(8,128)(2,1)} async-done(((bf16[16,32,2048]{2,1,0:T(8,128)(2,1)}), bf16[16,32,2048]{2,1,0:T(8,128)(2,1)}, u32[]{:S(2)}, u32[]{:S(2)}) %all-to-all-start.1) | async-done | bytes 2097184 | tf_op jit(solution)/shard_map/all_to_all | solution.py:79
  63.3 4.8 %all-to-all-start = ((bf16[16,32,2048]{2,1,0:T(8,128)(2,1)}), bf16[16,32,2048]{2,1,0:T(8,128)(2,1)}, u32[]{:S(2)}, u32[]{:S(2)}) async-start(bf16[16,32,2048]{2,1,0:T(8,128)(2,1)} %bitcast.78), calls=%async_computation | async-start | bytes 4194304 | tf_op jit(solution)/shard_map/all_to_all | solution.py:79
  68.1 8.5 %fusion.2 = f32[512,1536]{1,0:T(8,128)} fusion(bf16[512,2048]{1,0:T(8,128)(2,1)} %bitcast.5, bf16[1,2048,1536]{2,1,0:T(8,128)(2,1)} %param.8), kind=kOutput, calls=%fused_computation.4 | convolution fusion | flops 3221225472 | bytes 11534336 | tf_op jit(solution)/shard_map/dot_general | solution.py:86
  76.7 40.6 %all-to-all-done = bf16[16,32,2048]{2,1,0:T(8,128)(2,1)} async-done(((bf16[16,32,2048]{2,1,0:T(8,128)(2,1)}), bf16[16,32,2048]{2,1,0:T(8,128)(2,1)}, u32[]{:S(2)}, u32[]{:S(2)}) %all-to-all-start) | async-done | bytes 2097184 | tf_op jit(solution)/shard_map/all_to_all | solution.py:79
  117.3 6.2 %convolution_convert_fusion.1 = bf16[2048,768]{0,1:T(8,128)(2,1)} fusion(bf16[512,2048]{1,0:T(8,128)(2,1)} %bitcast.2, f32[512,1536]{1,0:T(8,128)} %fusion.2), kind=kOutput, calls=%fused_computation.6 | convolution fusion | flops 1614544896 | bytes 8388608 | tf_op jit(solution)/shard_map/dot_general | solution.py:108
  123.5 3.9 %multiply_convert_fusion.2 = (bf16[512,768]{1,0:T(8,128)(2,1)S(1)}, bf16[512,768]{1,0:T(8,128)(2,1)S(1)}) fusion(f32[512,1536]{1,0:T(8,128)S(1)} %copy-done.4, bf16[512,2048]{1,0:T(8,128)(2,1)} %bitcast.2, bf16[1,2048,768]{2,1,0:T(8,128)(2,1)S(1)} %copy-done), kind=kOutput, calls=%fused_computation.24 | convolution fusion | flops 1615724544 | bytes 9961472 | tf_op jit(solution)/shard_map/dot_general | solution.py:92
  127.4 4.7 %fusion.6 = bf16[512,2048]{1,0:T(8,128)(2,1)} fusion(bf16[1,2048,1536]{2,1,0:T(8,128)(2,1)S(1)} %bitcast.84, bf16[512,768]{1,0:T(8,128)(2,1)S(1)} %get-tuple-element.9, bf16[512,768]{1,0:T(8,128)(2,1)S(1)} %get-tuple-element.8), kind=kOutput, calls=%fused_computation.11 | convolution fusion | flops 3225419776 | bytes 9961472 | tf_op jit(solution)/shard_map/dot_general | solution.py:96
  132.1 7.0 %convolution_convert_fusion = bf16[2048,1536]{0,1:T(8,128)(2,1)} fusion(bf16[512,2048]{1,0:T(8,128)(2,1)} %bitcast.5, bf16[512,768]{1,0:T(8,128)(2,1)S(1)} %get-tuple-element.9, bf16[512,768]{1,0:T(8,128)(2,1)S(1)} %get-tuple-element.8), kind=kOutput, calls=%fused_computation.1 | convolution fusion | flops 3227516928 | bytes 9961472 | tf_op jit(solution)/shard_map/dot_general | solution.py:105
  139.1 5.1 %all-to-all-start.2 = ((bf16[16,32,2048]{2,1,0:T(8,128)(2,1)}), bf16[16,32,2048]{2,1,0:T(8,128)(2,1)}, u32[]{:S(2)}, u32[]{:S(2)}) async-start(bf16[16,32,2048]{2,1,0:T(8,128)(2,1)} %bitcast.80), calls=%async_computation.2 | async-start | bytes 4194304 | tf_op jit(solution)/shard_map/all_to_all | solution.py:99
  144.2 7.0 %pad_maximum_fusion = bf16[2048,2304]{0,1:T(8,128)(2,1)} fusion(bf16[2048,768]{0,1:T(8,128)(2,1)S(1)} %copy-done.3, bf16[2048,1536]{0,1:T(8,128)(2,1)} %convolution_convert_fusion), kind=kLoop, calls=%fused_computation | loop fusion | flops 18874368 | bytes 18874368 | tf_op jit(solution)/shard_map/concatenate | solution.py:111
  151.1 12.7 %copy.20 = bf16[2048,2304]{1,0:T(8,128)(2,1)} copy(bf16[2048,2304]{0,1:T(8,128)(2,1)} %pad_maximum_fusion) | data formatting | bytes 18874368 | tf_op jit(solution)/shard_map/concatenate | solution.py:111
  163.9 3.7 %slice_bitcast_fusion.2 = (bf16[4,4,32,2304]{3,2,1,0:T(8,128)(2,1)S(1)}, bf16[4,4,32,2304]{3,2,1,0:T(8,128)(2,1)S(1)}, bf16[4,4,32,2304]{3,2,1,0:T(8,128)(2,1)S(1)}) fusion(bf16[4,4,4,32,2304]{4,3,2,1,0:T(8,128)(2,1)} %bitcast.74), kind=kLoop, calls=%fused_computation.15 | loop fusion | bytes 14155776 | tf_op jit(solution)/shard_map/squeeze | solution.py:57
  167.6 0.1 broadcast_select_fusion
  167.7 3.1 %collective-permute-start.12 = (bf16[4,2,32,2304]{3,2,1,0:T(8,128)(2,1)S(1)}, bf16[4,2,32,2304]{3,2,1,0:T(8,128)(2,1)S(1)}, u32[]{:S(2)}, u32[]{:S(2)}) collective-permute-start(bf16[4,2,32,2304]{3,2,1,0:T(8,128)(2,1)S(1)} %broadcast_select_fusion), channel_id=1, source_target_pairs={{0,48},{16,32},{32,16},{48,0},{64,112},{80,96},{96,80},{112,64},{1... | collective-permute-start | bytes 3538952 | tf_op jit(solution)/shard_map/ppermute | solution.py:64
  170.8 0.1 broadcast_select_fusion.1
  171.0 0.2 collective-permute-start.8
  171.2 0.2 broadcast_select_fusion.2
  171.4 0.6 collective-permute-start
  172.0 0.1 select_bitcast_fusion
  172.1 2.2 collective-permute-start.4
  174.4 23.0 %collective-permute-done.12 = bf16[4,2,32,2304]{3,2,1,0:T(8,128)(2,1)S(1)} collective-permute-done((bf16[4,2,32,2304]{3,2,1,0:T(8,128)(2,1)S(1)}, bf16[4,2,32,2304]{3,2,1,0:T(8,128)(2,1)S(1)}, u32[]{:S(2)}, u32[]{:S(2)}) %collective-permute-start.12) | collective-permute-done | bytes 1179680 | tf_op jit(solution)/shard_map/ppermute | solution.py:64
  197.3 0.4 add_convert_fusion
  197.7 0.1 broadcast_select_fusion.3
  197.8 0.4 collective-permute-start.13
  198.2 0.8 collective-permute-done.8
  199.0 0.4 add_convert_fusion.1
  199.4 0.1 broadcast_select_fusion.4
  199.5 2.0 collective-permute-start.9
  201.5 1.1 add_convert_fusion.2
  202.6 0.1 broadcast_select_fusion.5
  202.6 1.0 collective-permute-start.5
  203.7 1.8 collective-permute-start.1
  205.6 7.2 %collective-permute-done.13 = bf16[4,1,32,2304]{3,2,1,0:T(8,128)(2,1)S(1)} collective-permute-done((bf16[4,1,32,2304]{3,2,1,0:T(8,128)(2,1)S(1)}, bf16[4,1,32,2304]{3,2,1,0:T(8,128)(2,1)S(1)}, u32[]{:S(2)}, u32[]{:S(2)}) %collective-permute-start.13) | collective-permute-done | bytes 589856 | tf_op jit(solution)/shard_map/ppermute | solution.py:64
  212.7 0.2 add_convert_fusion.3
  213.0 1.6 collective-permute-start.14
  214.6 0.7 collective-permute-done.9
  215.2 0.2 add_convert_fusion.4
  215.5 1.3 collective-permute-start.10
  216.8 1.1 collective-permute-done.5
  217.9 0.2 add_convert_fusion.5
  218.2 1.8 collective-permute-start.6
  220.0 0.1 collective-permute-done.1
  220.1 0.2 add_convert_fusion.6
  220.4 1.8 collective-permute-start.2
  222.2 2.2 collective-permute-done.14
  224.4 0.1 add_convert_fusion.7
  224.5 2.6 %collective-permute-start.15 = (bf16[1,1,32,2304]{3,2,1,0:T(8,128)(2,1)S(1)}, bf16[1,1,32,2304]{3,2,1,0:T(8,128)(2,1)S(1)}, u32[]{:S(2)}, u32[]{:S(2)}) collective-permute-start(bf16[1,1,32,2304]{3,2,1,0:T(8,128)(2,1)S(1)} %broadcast_select_fusion.11), channel_id=1, source_target_pairs={{0,64},{16,80},{32,96},{48,112},{64,0},{80,16},{96,32},{112,48},{1... | collective-permute-start | bytes 442376 | tf_op jit(solution)/shard_map/ppermute | solution.py:64
  227.1 0.1 add_convert_fusion.8
  227.2 1.6 collective-permute-start.11
  228.8 0.1 add_convert_fusion.9
  229.0 1.2 collective-permute-start.7
  230.2 0.1 add_convert_fusion.10
  230.3 1.0 collective-permute-start.3
  231.4 1.1 collective-permute-done.11
  232.5 1.7 collective-permute-done.7
  234.2 2.5 %collective-permute-done.3 = bf16[1,1,32,2304]{3,2,1,0:T(8,128)(2,1)S(1)} collective-permute-done((bf16[1,1,32,2304]{3,2,1,0:T(8,128)(2,1)S(1)}, bf16[1,1,32,2304]{3,2,1,0:T(8,128)(2,1)S(1)}, u32[]{:S(2)}, u32[]{:S(2)}) %collective-permute-start.3) | collective-permute-done | bytes 147488 | tf_op jit(solution)/shard_map/ppermute | solution.py:64
  236.8 0.7 maximum_bitcast_fusion
  237.5 0.8 slice_bitcast_fusion.6
  238.3 3.3 %convolution_convert_fusion.4 = bf16[160,2048]{1,0:T(8,128)(2,1)} fusion(bf16[512,2048]{1,0:T(8,128)(2,1)} %bitcast.8, s32[160]{0:T(256)S(1)} %multiply_add_fusion), kind=kOutput, calls=%fused_computation.12 | convolution fusion | flops 335953920 | bytes 2753152 | tf_op jit(solution)/shard_map/dot_general | solution.py:102
  (36 shorter events, 0.6 us)
Async XLA Ops:
  0.6 122.9 %copy-start = (bf16[1,2048,768]{2,1,0:T(8,128)(2,1)S(1)}, bf16[1,2048,768]{2,1,0:T(8,128)(2,1)}, u32[]{:S(2)}) copy-start(bf16[1,2048,768]{2,1,0:T(8,128)(2,1)} %param.9) | copy-start | bytes 9437188
  5.4 57.9 %all-to-all-start.1 = ((bf16[16,32,2048]{2,1,0:T(8,128)(2,1)}), bf16[16,32,2048]{2,1,0:T(8,128)(2,1)}, u32[]{:S(2)}, u32[]{:S(2)}) async-start(bf16[16,32,2048]{2,1,0:T(8,128)(2,1)} %bitcast.79), calls=%async_computation.1 | async-start | bytes 4194304 | tf_op jit(solution)/shard_map/all_to_all | solution.py:79
  63.3 54.0 %all-to-all-start = ((bf16[16,32,2048]{2,1,0:T(8,128)(2,1)}), bf16[16,32,2048]{2,1,0:T(8,128)(2,1)}, u32[]{:S(2)}, u32[]{:S(2)}) async-start(bf16[16,32,2048]{2,1,0:T(8,128)(2,1)} %bitcast.78), calls=%async_computation | async-start | bytes 4194304 | tf_op jit(solution)/shard_map/all_to_all | solution.py:79
  117.3 6.2 %copy-start.4 = (f32[512,1536]{1,0:T(8,128)S(1)}, f32[512,1536]{1,0:T(8,128)}, u32[]{:S(2)}) copy-start(f32[512,1536]{1,0:T(8,128)} %fusion.2) | copy-start | bytes 9437188
  117.3 10.1 %slice-start = ((s8[6291456]{0:T(1024)(128)(4,1)}), s8[4194304]{0:T(1024)(128)(4,1)S(1)}, s32[]{:S(2)}) async-start(s8[6291456]{0:T(1024)(128)(4,1)} %bitcast.83), calls=%async_computation.3 | async-start | bytes 8388608
  123.5 3.9 %slice-start.1 = ((s8[6291456]{0:T(1024)(128)(4,1)}), s8[2097152]{0:T(1024)(128)(4,1)S(1)}, s32[]{:S(2)}) async-start(s8[6291456]{0:T(1024)(128)(4,1)} %bitcast.83), calls=%async_computation.4 | async-start | bytes 4194304
  139.1 5.1 %copy-start.3 = (bf16[2048,768]{0,1:T(8,128)(2,1)S(1)}, bf16[2048,768]{0,1:T(8,128)(2,1)}, u32[]{:S(2)}) copy-start(bf16[2048,768]{0,1:T(8,128)(2,1)} %convolution_convert_fusion.1) | copy-start | bytes 9437188
  139.1 99.2 %all-to-all-start.2 = ((bf16[16,32,2048]{2,1,0:T(8,128)(2,1)}), bf16[16,32,2048]{2,1,0:T(8,128)(2,1)}, u32[]{:S(2)}, u32[]{:S(2)}) async-start(bf16[16,32,2048]{2,1,0:T(8,128)(2,1)} %bitcast.80), calls=%async_computation.2 | async-start | bytes 4194304 | tf_op jit(solution)/shard_map/all_to_all | solution.py:99
  163.9 7.3 %copy-start.2 = (bf16[2048,2304]{1,0:T(8,128)(2,1)S(1)}, bf16[2048,2304]{1,0:T(8,128)(2,1)}, u32[]{:S(2)}) copy-start(bf16[2048,2304]{1,0:T(8,128)(2,1)} %copy.20) | copy-start | bytes 28311556
  167.7 29.6 %collective-permute-start.12 = (bf16[4,2,32,2304]{3,2,1,0:T(8,128)(2,1)S(1)}, bf16[4,2,32,2304]{3,2,1,0:T(8,128)(2,1)S(1)}, u32[]{:S(2)}, u32[]{:S(2)}) collective-permute-start(bf16[4,2,32,2304]{3,2,1,0:T(8,128)(2,1)S(1)} %broadcast_select_fusion), channel_id=1, source_target_pairs={{0,48},{16,32},{32,16},{48,0},{64,112},{80,96},{96,80},{112,64},{1... | collective-permute-start | bytes 3538952 | tf_op jit(solution)/shard_map/ppermute | solution.py:64
  171.0 28.0 %collective-permute-start.8 = (bf16[4,2,32,2304]{3,2,1,0:T(8,128)(2,1)S(1)}, bf16[4,2,32,2304]{3,2,1,0:T(8,128)(2,1)S(1)}, u32[]{:S(2)}, u32[]{:S(2)}) collective-permute-start(bf16[4,2,32,2304]{3,2,1,0:T(8,128)(2,1)S(1)} %broadcast_select_fusion.1), channel_id=1, source_target_pairs={{0,16},{16,0},{32,48},{48,32},{64,80},{80,64},{96,112},{112,96},{1... | collective-permute-start | bytes 3538952 | tf_op jit(solution)/shard_map/ppermute | solution.py:64
  171.4 30.1 %collective-permute-start = (bf16[2,4,32,2304]{3,2,1,0:T(8,128)(2,1)S(1)}, bf16[2,4,32,2304]{3,2,1,0:T(8,128)(2,1)S(1)}, u32[]{:S(2)}, u32[]{:S(2)}) collective-permute-start(bf16[2,4,32,2304]{3,2,1,0:T(8,128)(2,1)S(1)} %broadcast_select_fusion.2), channel_id=1, source_target_pairs={{0,64},{16,80},{32,96},{48,112},{64,0},{80,16},{96,32},{112,48},{1... | collective-permute-start | bytes 3538952 | tf_op jit(solution)/shard_map/ppermute | solution.py:64
  172.1 29.4 %collective-permute-start.4 = (bf16[2,4,32,2304]{3,2,1,0:T(8,128)(2,1)S(1)}, bf16[2,4,32,2304]{3,2,1,0:T(8,128)(2,1)S(1)}, u32[]{:S(2)}, u32[]{:S(2)}) collective-permute-start(bf16[2,4,32,2304]{3,2,1,0:T(8,128)(2,1)S(1)} %select_bitcast_fusion), channel_id=1, source_target_pairs={{0,192},{16,208},{32,224},{48,240},{64,128},{80,144},{96,160},{112... | collective-permute-start | bytes 3538952 | tf_op jit(solution)/shard_map/ppermute | solution.py:64
  197.8 14.9 %collective-permute-start.13 = (bf16[4,1,32,2304]{3,2,1,0:T(8,128)(2,1)S(1)}, bf16[4,1,32,2304]{3,2,1,0:T(8,128)(2,1)S(1)}, u32[]{:S(2)}, u32[]{:S(2)}) collective-permute-start(bf16[4,1,32,2304]{3,2,1,0:T(8,128)(2,1)S(1)} %broadcast_select_fusion.3), channel_id=1, source_target_pairs={{0,16},{16,0},{32,48},{48,32},{64,80},{80,64},{96,112},{112,96},{1... | collective-permute-start | bytes 1769480 | tf_op jit(solution)/shard_map/ppermute | solution.py:64
  199.5 15.8 %collective-permute-start.9 = (bf16[4,1,32,2304]{3,2,1,0:T(8,128)(2,1)S(1)}, bf16[4,1,32,2304]{3,2,1,0:T(8,128)(2,1)S(1)}, u32[]{:S(2)}, u32[]{:S(2)}) collective-permute-start(bf16[4,1,32,2304]{3,2,1,0:T(8,128)(2,1)S(1)} %broadcast_select_fusion.4), channel_id=1, source_target_pairs={{0,48},{16,32},{32,16},{48,0},{64,112},{80,96},{96,80},{112,64},{1... | collective-permute-start | bytes 1769480 | tf_op jit(solution)/shard_map/ppermute | solution.py:64
  202.6 15.2 %collective-permute-start.5 = (bf16[1,4,32,2304]{3,2,1,0:T(8,128)(2,1)S(1)}, bf16[1,4,32,2304]{3,2,1,0:T(8,128)(2,1)S(1)}, u32[]{:S(2)}, u32[]{:S(2)}) collective-permute-start(bf16[1,4,32,2304]{3,2,1,0:T(8,128)(2,1)S(1)} %broadcast_select_fusion.5), channel_id=1, source_target_pairs={{0,64},{16,80},{32,96},{48,112},{64,0},{80,16},{96,32},{112,48},{1... | collective-permute-start | bytes 1769480 | tf_op jit(solution)/shard_map/ppermute | solution.py:64
  203.7 16.4 %collective-permute-start.1 = (bf16[1,4,32,2304]{3,2,1,0:T(8,128)(2,1)S(1)}, bf16[1,4,32,2304]{3,2,1,0:T(8,128)(2,1)S(1)}, u32[]{:S(2)}, u32[]{:S(2)}) collective-permute-start(bf16[1,4,32,2304]{3,2,1,0:T(8,128)(2,1)S(1)} %broadcast_select_fusion.6), channel_id=1, source_target_pairs={{0,192},{16,208},{32,224},{48,240},{64,128},{80,144},{96,160},{112... | collective-permute-start | bytes 1769480 | tf_op jit(solution)/shard_map/ppermute | solution.py:64
  213.0 11.3 %collective-permute-start.14 = (bf16[2,1,32,2304]{3,2,1,0:T(8,128)(2,1)S(1)}, bf16[2,1,32,2304]{3,2,1,0:T(8,128)(2,1)S(1)}, u32[]{:S(2)}, u32[]{:S(2)}) collective-permute-start(bf16[2,1,32,2304]{3,2,1,0:T(8,128)(2,1)S(1)} %broadcast_select_fusion.7), channel_id=1, source_target_pairs={{0,192},{16,208},{32,224},{48,240},{64,128},{80,144},{96,160},{112... | collective-permute-start | bytes 884744 | tf_op jit(solution)/shard_map/ppermute | solution.py:64
  215.5 11.6 %collective-permute-start.10 = (bf16[2,1,32,2304]{3,2,1,0:T(8,128)(2,1)S(1)}, bf16[2,1,32,2304]{3,2,1,0:T(8,128)(2,1)S(1)}, u32[]{:S(2)}, u32[]{:S(2)}) collective-permute-start(bf16[2,1,32,2304]{3,2,1,0:T(8,128)(2,1)S(1)} %broadcast_select_fusion.8), channel_id=1, source_target_pairs={{0,64},{16,80},{32,96},{48,112},{64,0},{80,16},{96,32},{112,48},{1... | collective-permute-start | bytes 884744 | tf_op jit(solution)/shard_map/ppermute | solution.py:64
  218.2 10.7 %collective-permute-start.6 = (bf16[1,2,32,2304]{3,2,1,0:T(8,128)(2,1)S(1)}, bf16[1,2,32,2304]{3,2,1,0:T(8,128)(2,1)S(1)}, u32[]{:S(2)}, u32[]{:S(2)}) collective-permute-start(bf16[1,2,32,2304]{3,2,1,0:T(8,128)(2,1)S(1)} %broadcast_select_fusion.9), channel_id=1, source_target_pairs={{0,48},{16,32},{32,16},{48,0},{64,112},{80,96},{96,80},{112,64},{1... | collective-permute-start | bytes 884744 | tf_op jit(solution)/shard_map/ppermute | solution.py:64
  220.4 9.8 %collective-permute-start.2 = (bf16[1,2,32,2304]{3,2,1,0:T(8,128)(2,1)S(1)}, bf16[1,2,32,2304]{3,2,1,0:T(8,128)(2,1)S(1)}, u32[]{:S(2)}, u32[]{:S(2)}) collective-permute-start(bf16[1,2,32,2304]{3,2,1,0:T(8,128)(2,1)S(1)} %broadcast_select_fusion.10), channel_id=1, source_target_pairs={{0,16},{16,0},{32,48},{48,32},{64,80},{80,64},{96,112},{112,96},{1... | collective-permute-start | bytes 884744 | tf_op jit(solution)/shard_map/ppermute | solution.py:64
  224.5 6.8 %collective-permute-start.15 = (bf16[1,1,32,2304]{3,2,1,0:T(8,128)(2,1)S(1)}, bf16[1,1,32,2304]{3,2,1,0:T(8,128)(2,1)S(1)}, u32[]{:S(2)}, u32[]{:S(2)}) collective-permute-start(bf16[1,1,32,2304]{3,2,1,0:T(8,128)(2,1)S(1)} %broadcast_select_fusion.11), channel_id=1, source_target_pairs={{0,64},{16,80},{32,96},{48,112},{64,0},{80,16},{96,32},{112,48},{1... | collective-permute-start | bytes 442376 | tf_op jit(solution)/shard_map/ppermute | solution.py:64
  227.2 5.2 %collective-permute-start.11 = (bf16[1,1,32,2304]{3,2,1,0:T(8,128)(2,1)S(1)}, bf16[1,1,32,2304]{3,2,1,0:T(8,128)(2,1)S(1)}, u32[]{:S(2)}, u32[]{:S(2)}) collective-permute-start(bf16[1,1,32,2304]{3,2,1,0:T(8,128)(2,1)S(1)} %broadcast_select_fusion.12), channel_id=1, source_target_pairs={{0,192},{16,208},{32,224},{48,240},{64,128},{80,144},{96,160},{112... | collective-permute-start | bytes 442376 | tf_op jit(solution)/shard_map/ppermute | solution.py:64
  229.0 5.2 %collective-permute-start.7 = (bf16[1,1,32,2304]{3,2,1,0:T(8,128)(2,1)S(1)}, bf16[1,1,32,2304]{3,2,1,0:T(8,128)(2,1)S(1)}, u32[]{:S(2)}, u32[]{:S(2)}) collective-permute-start(bf16[1,1,32,2304]{3,2,1,0:T(8,128)(2,1)S(1)} %broadcast_select_fusion.13), channel_id=1, source_target_pairs={{0,16},{16,0},{32,48},{48,32},{64,80},{80,64},{96,112},{112,96},{1... | collective-permute-start | bytes 442376 | tf_op jit(solution)/shard_map/ppermute | solution.py:64
  230.3 6.4 %collective-permute-start.3 = (bf16[1,1,32,2304]{3,2,1,0:T(8,128)(2,1)S(1)}, bf16[1,1,32,2304]{3,2,1,0:T(8,128)(2,1)S(1)}, u32[]{:S(2)}, u32[]{:S(2)}) collective-permute-start(bf16[1,1,32,2304]{3,2,1,0:T(8,128)(2,1)S(1)} %broadcast_select_fusion.14), channel_id=1, source_target_pairs={{0,48},{16,32},{32,16},{48,0},{64,112},{80,96},{96,80},{112,64},{1... | collective-permute-start | bytes 442376 | tf_op jit(solution)/shard_map/ppermute | solution.py:64
  237.5 4.1 %copy-start.1 = (bf16[1,2048,768]{2,1,0:T(8,128)(2,1)S(1)}, bf16[1,2048,768]{2,1,0:T(8,128)(2,1)}, u32[]{:S(2)}) copy-start(bf16[1,2048,768]{2,1,0:T(8,128)(2,1)} %param.9) | copy-start | bytes 9437188

commit v3 on v1

v3 whole, which is shorter than its diff:
```python
import jax
import jax.numpy as jnp
from jax import lax
from jax.experimental import pallas as pl
from jax.experimental.pallas import tpu as pltpu
from jax.sharding import PartitionSpec as P

SLOTS = 32
SIDE = 4
VMEM_LIMIT = 48 * 1024 * 1024


def slot_table(routed, num_experts):
    rows = routed.shape[0]
    places = jnp.arange(rows, dtype=jnp.int32)
    same = (routed[:, None] == routed[None, :]) & (places[:, None] < places[None, :])
    slots = jnp.sum(same.astype(jnp.int32), axis=0)
    target = routed * SLOTS + slots
    spots = jnp.arange(num_experts * SLOTS, dtype=jnp.int32)
    return (spots[:, None] == target[None, :]).astype(jnp.bfloat16)


def dgate_up_kernel(w_ref, dy_ref, a_ref, s_ref, out_ref):
    dhidden = lax.dot_general(
        w_ref[...], dy_ref[...], (((1,), (1,)), ((), ())), preferred_element_type=jnp.float32
    )
    out_ref[0] = (dhidden * a_ref[...]).astype(jnp.bfloat16)
    out_ref[1] = (dhidden * s_ref[...]).astype(jnp.bfloat16)


def make_dgate_up(w_out_t, rows_dy, slope, silu):
    ff, width = w_out_t.shape
    rows = rows_dy.shape[0]
    tile = 256
    return pl.pallas_call(
        dgate_up_kernel,
        grid=(ff // tile,),
        in_specs=[
            pl.BlockSpec((tile, width), lambda i: (i, 0)),
            pl.BlockSpec((rows, width), lambda i: (0, 0)),
            pl.BlockSpec((tile, rows), lambda i: (i, 0)),
            pl.BlockSpec((tile, rows), lambda i: (i, 0)),
        ],
        out_specs=pl.BlockSpec((2, tile, rows), lambda i: (0, i, 0)),
        out_shape=jax.ShapeDtypeStruct((2, ff, rows), jnp.bfloat16),
        compiler_params=pltpu.CompilerParams(vmem_limit_bytes=VMEM_LIMIT),
        cost_estimate=pl.CostEstimate(
            flops=2 * ff * rows * width, bytes_accessed=10 * ff * rows + 4 * rows * width, transcendentals=0
        ),
        name="dgate_up",
    )(w_out_t, rows_dy, slope, silu)


def drows_kernel(g_ref, w_ref, out_ref, turned):
    @pl.when(pl.program_id(0) == 0)
    def _():
        turned[...] = g_ref[...].T

    out_ref[...] = lax.dot_general(
        turned[...], w_ref[...], (((1,), (1,)), ((), ())), preferred_element_type=jnp.float32
    ).astype(jnp.bfloat16)


def make_drows(dgu_t, w_in):
    ff2, rows = dgu_t.shape
    width = w_in.shape[0]
    tile = 512
    return pl.pallas_call(
        drows_kernel,
        grid=(width // tile,),
        in_specs=[
            pl.BlockSpec((ff2, rows), lambda i: (0, 0)),
            pl.BlockSpec((tile, ff2), lambda i: (i, 0)),
        ],
        out_specs=pl.BlockSpec((rows, tile), lambda i: (0, i)),
        out_shape=jax.ShapeDtypeStruct((rows, width), jnp.bfloat16),
        scratch_shapes=[pltpu.VMEM((rows, ff2), jnp.bfloat16)],
        compiler_params=pltpu.CompilerParams(vmem_limit_bytes=VMEM_LIMIT),
        cost_estimate=pl.CostEstimate(
            flops=2 * ff2 * rows * width, bytes_accessed=2 * ff2 * (rows + width), transcendentals=0
        ),
        name="drows",
    )(dgu_t, w_in)


def partial_kernel(parts, table, *refs):
    out_ref = refs[-1]
    at = 0
    row = 0
    for start, count in parts:
        left = refs[at][start : start + count, :]
        right = jnp.concatenate([refs[at + 1 + i][...] for i in range(SIDE)], axis=1)
        out_ref[row : row + count, :] = jnp.dot(
            left, right, preferred_element_type=jnp.float32
        ).astype(jnp.bfloat16)
        at += 1 + SIDE
        row += count


def make_partial(table, pieces, name):
    blocks = table.shape[0]
    lane = 128
    specs, operands, parts = [], [], []
    for left, block, index, start, count, right in pieces:
        rows = left.shape[1]
        specs.append(pl.BlockSpec((block, rows), lambda i, t, index=index: (index, 0)))
        operands.append(left)
        for k in range(SIDE):
            specs.append(pl.BlockSpec((rows, lane), lambda i, t, k=k: (0, t[i * SIDE + k])))
            operands.append(right)
        parts.append((start, count))
    total = sum(count for _, count in parts)
    return pl.pallas_call(
        lambda table, *refs: partial_kernel(parts, table, *refs),
        grid_spec=pltpu.PrefetchScalarGridSpec(
            num_scalar_prefetch=1,
            grid=(blocks // SIDE,),
            in_specs=specs,
            out_specs=pl.BlockSpec((total, SIDE * lane), lambda i, t: (0, i)),
        ),
        out_shape=jax.ShapeDtypeStruct((total, blocks * lane), jnp.bfloat16),
        compiler_params=pltpu.CompilerParams(vmem_limit_bytes=VMEM_LIMIT),
        cost_estimate=pl.CostEstimate(
            flops=2 * total * rows * blocks * lane,
            bytes_accessed=2 * (total * rows + rows * blocks * lane + total * blocks * lane),
            transcendentals=0,
        ),
        name=name,
    )(table, *operands)


def pair_perm(axis, odd):
    def mate(i):
        return (3 - i) if odd else (i ^ 1)

    return [
        (x * SIDE + y, mate(x) * SIDE + y if axis == 0 else x * SIDE + mate(y))
        for x in range(SIDE)
        for y in range(SIDE)
    ]


FLOWS = ((0, False), (0, True), (1, False), (1, True))


def first_table(at, axis, odd):
    i = at[axis]
    minor = jnp.arange(SIDE, dtype=jnp.int32)

    def blocks(a, b):
        major = jnp.array([a, b], jnp.int32)
        ids = major[:, None] * SIDE + minor[None, :] if axis == 0 else minor[None, :] * SIDE + major[:, None]
        return ids.reshape(-1)

    low, high = (blocks(0, 1), blocks(2, 3)) if odd else (blocks(0, 3), blocks(1, 2))
    mine_low = (i < 2) if odd else ((i == 0) | (i == 3))
    return jnp.where(mine_low, high, low), jnp.where(mine_low, low, high)


def halves(block, at, axis, odd, step):
    i = at[axis]
    n = block.shape[1]
    if step % 2 == 1:
        low, high = block[:, : n // 2], block[:, n // 2 :]
        mine_low = (i % 2 == 0) if odd else (i < 2)
    else:
        q = n // 4
        if odd:
            low, high = block[:, : 2 * q], block[:, 2 * q :]
            mine_low = i < 2
        else:
            low = jnp.concatenate([block[:, :q], block[:, 3 * q :]], axis=1)
            high = block[:, q : 3 * q]
            mine_low = (i == 0) | (i == 3)
    return jnp.where(mine_low, high, low), jnp.where(mine_low, low, high)


def local(tokens, out_grads, expert_ids, w_gate_up, w_down_t):
    num_experts = lax.axis_size("expert")
    width = tokens.shape[1]
    ff = w_down_t.shape[2]
    rows = num_experts * SLOTS
    dispatch = slot_table(expert_ids[:, 0], num_experts)

    def send(values):
        slots = jnp.dot(dispatch, values, preferred_element_type=jnp.float32).astype(jnp.bfloat16)
        slots = slots.reshape(num_experts, SLOTS, width)
        got = lax.all_to_all(slots, "expert", split_axis=0, concat_axis=0, tiled=True)
        return got.reshape(rows, width)

    rows_x = send(tokens)
    rows_dy = send(out_grads)
    w_in = w_gate_up[0]
    w_out_t = w_down_t[0].T

    gate_up = lax.dot_general(
        w_in, rows_x, (((0,), (1,)), ((), ())), preferred_element_type=jnp.float32
    )
    gate = gate_up[:ff]
    upper = gate_up[ff:]
    sig = jax.nn.sigmoid(gate)
    silu = gate * sig
    hidden = (silu * upper).astype(jnp.bfloat16)
    slope = upper * sig * (1.0 + gate * (1.0 - sig))

    me = lax.axis_index("dp")
    at = (me // SIDE, me % SIDE)
    tables = [first_table(at, axis, odd) for axis, odd in FLOWS]

    dgu = make_dgate_up(w_out_t, rows_dy, slope, silu).reshape(2 * ff, rows)
    per = 3 * ff // 4
    left = 2 * ff - 2 * per
    pieces = (
        [(dgu, per, 0, 0, per, rows_x)],
        [(dgu, per, 1, 0, per, rows_x)],
        [(dgu, left, 2 * per // left, 0, left, rows_x), (hidden, per - left, 0, 0, per - left, rows_dy)],
        [(hidden, ff, 0, per - left, per, rows_dy)],
    )
    blocks = [None] * 4
    for f in (3, 0, 1, 2):
        axis, odd = FLOWS[f]
        give = make_partial(tables[f][0], pieces[f], "give")
        got = lax.ppermute(give, "dp", pair_perm(axis, odd))
        keep = make_partial(tables[f][1], pieces[f], "keep")
        blocks[f] = (keep.astype(jnp.float32) + got.astype(jnp.float32)).astype(jnp.bfloat16)

    drows = make_drows(dgu, w_in)
    returned = lax.all_to_all(
        drows.reshape(num_experts, SLOTS, width), "expert", split_axis=0, concat_axis=0, tiled=True
    ).reshape(rows, width)
    token_grads = lax.dot_general(
        dispatch, returned, (((0,), (0,)), ((), ())), preferred_element_type=jnp.float32
    ).astype(jnp.bfloat16)

    for step in range(1, 4):
        for f, (first_axis, first_odd) in enumerate(FLOWS):
            axis = first_axis if step < 2 else 1 - first_axis
            odd = first_odd if step % 2 == 0 else not first_odd
            give, keep = halves(blocks[f], at, axis, first_odd, step)
            got = lax.ppermute(give, "dp", pair_perm(axis, odd))
            blocks[f] = (keep.astype(jnp.float32) + got.astype(jnp.float32)).astype(jnp.bfloat16)
    summed = jnp.concatenate(blocks, axis=0).T
    return (token_grads, summed[None, :, : 2 * ff], summed[None, :, 2 * ff :])


def solution(mesh):
    return jax.shard_map(
        local,
        mesh=mesh,
        in_specs=(
            P(("dp", "expert"), None),
            P(("dp", "expert"), None),
            P(("dp", "expert"), None),
            P("expert", None, None),
            P("expert", None, None),
        ),
        out_specs=(P(("dp", "expert"), None), P("expert", "dp", None), P("expert", "dp", None)),
        check_vma=False,
    )
```

time: 307 us -> 218 us (0.71)
  waiting for transfers between devices: 181 us -> 104 us
  blocking collectives: 54.3 us -> 0 us
  Pallas kernels: 0 us -> 33.8 us
  matrix products: 40.8 us -> 12.7 us
  starting transfers between devices: 13.7 us -> 37.4 us
  local copies, waits for them, and re-layouts: 1.17 us -> 14.3 us
  between operations: 14.1 us -> 1.1 us
  other arithmetic: 1.65 us -> 13.5 us
    reduce_scatter x2 -> x0, waiting for transfers between devices: 94.1 us -> none  [the longest x1 90.1 us: local(): lax.psum_scatter(first, 'dp', scatter_dimension=0, tiled=True)[None]]
    all_to_all x1 -> x0, blocking collectives: 54.3 us -> none  [local(): lax.all_to_all(drows.reshape(num_experts, SLOTS, width), 'expert', split_...]
    pallas_call x0 -> x10, Pallas kernels: none -> 33.8 us  [the longest x8 22.6 us: make_partial(): pl.pallas_call(lambda table, *refs: partial_kernel(parts, table, *refs),...]
    dot_general x7 -> x3, matrix products: 39.4 us -> 9.67 us  [the longest x1 5.59 us: local(): lax.dot_general(w_in, rows_x, (((0,), (1,)), ((), ())), preferred_element...]
    ppermute x0 -> x16, waiting for transfers between devices: none -> 20.2 us  [local(): got = lax.ppermute(give, 'dp', pair_perm(axis, odd))]
    ppermute x0 -> x16, starting transfers between devices: none -> 18.9 us  [local(): got = lax.ppermute(give, 'dp', pair_perm(axis, odd))]
    unnamed x6 -> x31, local copies, waits for them, and re-layouts: 1.17 us -> 13.5 us
    convert_element_type x0 -> x17, other arithmetic: none -> 11.1 us  [the longest x16 8.57 us: local(): (keep.astype(jnp.float32) + got.astype(jnp.float32)).astype(jnp.bfloat16)]
  transfers between devices with their start and end apart: 4 -> 19, of which waited for: 4 -> 11; matrix products, arithmetic and copies ran while one was open for 10% -> 12% of each run, Pallas kernels for 0% -> 12%
where the time goes in v3:
time: 218 us; the launch traced here: 216 us
  waiting for transfers between devices  104 us (48%)
  starting transfers between devices  37.4 us (17%)
  Pallas kernels  33.8 us (16%)
  local copies, waits for them, and re-layouts  14.3 us (7%)
  other arithmetic  13.5 us (6%)
  matrix products  12.7 us (6%)
    all_to_all x2, waiting for transfers between devices, send(): lax.all_to_all(slots, 'expert', split_axis=0, concat_axis=0, tiled=True)  83.3 us
    pallas_call x8, Pallas kernels, make_partial(): pl.pallas_call(lambda table, *refs: partial_kernel(parts, table, *refs),...  22.6 us
    ppermute x16, waiting for transfers between devices, local(): got = lax.ppermute(give, 'dp', pair_perm(axis, odd))  20.2 us
    ppermute x16, starting transfers between devices, local(): got = lax.ppermute(give, 'dp', pair_perm(axis, odd))  18.9 us
    all_to_all x2, starting transfers between devices, send(): lax.all_to_all(slots, 'expert', split_axis=0, concat_axis=0, tiled=True)  13.6 us
    unnamed x31, local copies, waits for them, and re-layouts  13.5 us
    convert_element_type x16, other arithmetic, local(): (keep.astype(jnp.float32) + got.astype(jnp.float32)).astype(jnp.bfloat16)  8.57 us
    pallas_call x1, Pallas kernels, make_drows(): pl.pallas_call(drows_kernel, grid=(width // tile,), in_specs=[pl.BlockSpe...  6.49 us
  transfers between devices with their start and end apart: 19, of which 11 were waited for; matrix products, arithmetic and copies ran while one was open for 12% of the time, Pallas kernels for 12%

profile of v3, /device:TPU:2, one launch (start us, length us, event | category | flops | bytes accessed | tf_op | source)
XLA Modules:
  0.0 216.3 jit_solution(10656967050073675049)
XLA Ops:
  0.6 0.9 convert_reduce_fusion
  1.5 0.7 multiply_add_fusion
  2.2 2.1 convolution_convert_fusion
  4.3 8.7 %all-to-all-start.1 = ((bf16[16,32,2048]{2,1,0:T(8,128)(2,1)}), bf16[16,32,2048]{2,1,0:T(8,128)(2,1)S(1)}, u32[]{:S(2)}, u32[]{:S(2)}) async-start(bf16[16,32,2048]{2,1,0:T(8,128)(2,1)} %bitcast.61), calls=%async_computation.1 | async-start | bytes 4194304 | tf_op jit(solution)/shard_map/all_to_all | solution.py:188
  13.0 2.0 convolution_convert_fusion.1
  15.0 47.2 %all-to-all-done.1 = bf16[16,32,2048]{2,1,0:T(8,128)(2,1)S(1)} async-done(((bf16[16,32,2048]{2,1,0:T(8,128)(2,1)}), bf16[16,32,2048]{2,1,0:T(8,128)(2,1)S(1)}, u32[]{:S(2)}, u32[]{:S(2)}) %all-to-all-start.1) | async-done | bytes 2097184 | tf_op jit(solution)/shard_map/all_to_all | solution.py:188
  62.2 4.9 %all-to-all-start = ((bf16[16,32,2048]{2,1,0:T(8,128)(2,1)}), bf16[16,32,2048]{2,1,0:T(8,128)(2,1)}, u32[]{:S(2)}, u32[]{:S(2)}) async-start(bf16[16,32,2048]{2,1,0:T(8,128)(2,1)} %bitcast.60), calls=%async_computation | async-start | bytes 4194304 | tf_op jit(solution)/shard_map/all_to_all | solution.py:188
  67.3 4.7 %copy.20 = bf16[1,2048,768]{1,2,0:T(8,128)(2,1)} copy(bf16[1,2048,768]{2,1,0:T(8,128)(2,1)} %param.17) | data formatting | bytes 6291456 | tf_op args[4]
  72.0 5.6 %convolution_bitcast_fusion = f32[1536,512]{1,0:T(8,128)S(1)} fusion(bf16[512,2048]{1,0:T(8,128)(2,1)S(1)} %bitcast.26, bf16[1,2048,1536]{2,1,0:T(8,128)(2,1)} %param.16), kind=kOutput, calls=%fused_computation | convolution fusion | flops 3221225472 | bytes 11534336 | tf_op jit(solution)/shard_map/dot_general | solution.py:196
  77.6 2.6 %multiply_convert_fusion = (bf16[768,512]{1,0:T(8,128)(2,1)S(1)}, f32[768,512]{1,0:T(8,128)}, f32[768,512]{1,0:T(8,128)}) fusion(f32[1536,512]{1,0:T(8,128)S(1)} %convolution_bitcast_fusion), kind=kLoop, calls=%fused_computation.8 | loop fusion | flops 4325376 | bytes 7077888 | tf_op jit(solution)/shard_map/convert_element_type | solution.py:203
  80.2 36.2 %all-to-all-done = bf16[16,32,2048]{2,1,0:T(8,128)(2,1)} async-done(((bf16[16,32,2048]{2,1,0:T(8,128)(2,1)}), bf16[16,32,2048]{2,1,0:T(8,128)(2,1)}, u32[]{:S(2)}, u32[]{:S(2)}) %all-to-all-start) | async-done | bytes 2097184 | tf_op jit(solution)/shard_map/all_to_all | solution.py:188
  116.3 1.4 copy-done.6
  117.7 1.4 copy-done.7
  119.1 4.7 %dgate_up.1 = bf16[2,768,512]{2,1,0:T(8,128)(2,1)S(1)} custom-call(bf16[768,2048]{1,0:T(8,128)(2,1)} %bitcast.59, bf16[512,2048]{1,0:T(8,128)(2,1)} %bitcast.4.dy_ref.refs_6_.refs_7_.refs_8_.refs_9_.refs_1_.refs_2_.refs_3_.refs_4_, f32[768,512]{1,0:T(8,128)S(1)} %copy-done.6, f32[768,512]{1,0:T(8,128)S(1)} %copy-done.7), custom_call_target="tpu_custom_call" | custom-call | flops 1610612736 | bytes 8126464 | tf_op jit(solution)/shard_map/dgate_up/pallas_call | solution.py:35
  123.9 2.8 %give.4 = bf16[576,1024]{1,0:T(8,128)(2,1)} custom-call(s32[8]{0:T(128)S(1)} %select_n.216.table, bf16[1536,512]{1,0:T(8,128)(2,1)S(1)} %bitcast.51, bf16[512,2048]{1,0:T(8,128)(2,1)S(1)} %bitcast.27, bf16[512,2048]{1,0:T(8,128)(2,1)S(1)} %bitcast.28, bf16[512,2048]{1,0:T(8,128)(2,1)S(1)} %bitcast.29, bf16[512,2048]{1,0:T(8,128)(2,1)S(1)} %bitcast.30), custom_call_target="tpu_custom_call" | custom-call | flops 603979776 | bytes 2818048 | tf_op jit(solution)/shard_map/give/pallas_call | solution.py:113
  126.7 0.5 collective-permute-start
  128.0 1.4 copy-done.3
  129.4 2.7 %give.5 = bf16[576,1024]{1,0:T(8,128)(2,1)} custom-call(s32[8]{0:T(128)S(1)} %select_n.232.table, bf16[1536,512]{1,0:T(8,128)(2,1)S(1)} %bitcast.52, bf16[512,2048]{1,0:T(8,128)(2,1)S(1)} %bitcast.31, bf16[512,2048]{1,0:T(8,128)(2,1)S(1)} %bitcast.32, bf16[512,2048]{1,0:T(8,128)(2,1)S(1)} %bitcast.33, bf16[512,2048]{1,0:T(8,128)(2,1)S(1)} %bitcast.34), custom_call_target="tpu_custom_call" | custom-call | flops 603979776 | bytes 2818048 | tf_op jit(solution)/shard_map/give/pallas_call | solution.py:113
  132.1 2.1 collective-permute-start.4
  134.3 3.7 %give.6 = bf16[576,1024]{1,0:T(8,128)(2,1)} custom-call(s32[8]{0:T(128)S(1)} %select_n.246.table, bf16[1536,512]{1,0:T(8,128)(2,1)S(1)} %bitcast.53, bf16[512,2048]{1,0:T(8,128)(2,1)S(1)} %bitcast.38, bf16[512,2048]{1,0:T(8,128)(2,1)S(1)} %bitcast.36, bf16[512,2048]{1,0:T(8,128)(2,1)S(1)} %bitcast.37, bf16[512,2048]{1,0:T(8,128)(2,1)S(1)} %bitcast.35, ...), custom_call_target="tpu_custom_call" | custom-call | flops 603979776 | bytes 2818048 | tf_op jit(solution)/shard_map/give/pallas_call | solution.py:113
  138.0 1.6 collective-permute-start.8
  139.6 3.5 %give.7 = bf16[576,1024]{1,0:T(8,128)(2,1)} custom-call(s32[8]{0:T(128)S(1)} %select_n.260.table, bf16[768,512]{1,0:T(8,128)(2,1)S(1)} %get-tuple-element.9.refs_5_.refs_0_, bf16[512,2048]{1,0:T(8,128)(2,1)} %bitcast.4.dy_ref.refs_6_.refs_7_.refs_8_.refs_9_.refs_1_.refs_2_.refs_3_.refs_4_, ...), custom_call_target="tpu_custom_call" | custom-call | flops 603979776 | bytes 2818048 | tf_op jit(solution)/shard_map/give/pallas_call | solution.py:113
  143.1 2.2 %collective-permute-start.12 = (bf16[576,1024]{1,0:T(8,128)(2,1)}, bf16[576,1024]{1,0:T(8,128)(2,1)}, u32[]{:S(2)}, u32[]{:S(2)}) collective-permute-start(bf16[576,1024]{1,0:T(8,128)(2,1)} %give.7), channel_id=1, source_target_pairs={{0,48},{16,32},{32,16},{48,0},{64,112},{80,96},{96,80},{112,64},{1... | collective-permute-start | bytes 3538952 | tf_op jit(solution)/shard_map/ppermute | solution.py:223
  145.3 6.5 %drows.1 = bf16[512,2048]{1,0:T(8,128)(2,1)S(1)} custom-call(bf16[1536,512]{1,0:T(8,128)(2,1)S(1)} %bitcast.54, bf16[2048,1536]{1,0:T(8,128)(2,1)} %bitcast.64), custom_call_target="tpu_custom_call" | custom-call | flops 3221225472 | bytes 7864320 | tf_op jit(solution)/shard_map/drows/pallas_call | solution.py:68
  151.8 1.4 copy-done.8
  153.2 4.8 %all-to-all-start.2 = ((bf16[16,32,2048]{2,1,0:T(8,128)(2,1)}), bf16[16,32,2048]{2,1,0:T(8,128)(2,1)}, u32[]{:S(2)}, u32[]{:S(2)}) async-start(bf16[16,32,2048]{2,1,0:T(8,128)(2,1)} %bitcast.58), calls=%async_computation.2 | async-start | bytes 4194304 | tf_op jit(solution)/shard_map/all_to_all | solution.py:228
  158.0 1.4 copy-done.5
  159.4 2.0 keep.4
  161.4 2.0 keep.5
  163.4 3.0 %keep.6 = bf16[576,1024]{1,0:T(8,128)(2,1)S(1)} custom-call(s32[8]{0:T(128)S(1)} %select_n.244.table, bf16[1536,512]{1,0:T(8,128)(2,1)S(1)} %bitcast.57, bf16[512,2048]{1,0:T(8,128)(2,1)S(1)} %bitcast.47, bf16[512,2048]{1,0:T(8,128)(2,1)S(1)} %bitcast.48, bf16[512,2048]{1,0:T(8,128)(2,1)S(1)} %bitcast.49, bf16[512,2048]{1,0:T(8,128)(2,1)S(1)} %bitcast.50, ...), custom_call_target="tpu_custom_call" | custom-call | flops 603979776 | bytes 2818048 | tf_op jit(solution)/shard_map/keep/pallas_call | solution.py:113
  166.4 2.8 %keep.7 = bf16[576,1024]{1,0:T(8,128)(2,1)S(1)} custom-call(s32[8]{0:T(128)S(1)} %select_n.258.table, bf16[768,512]{1,0:T(8,128)(2,1)S(1)} %get-tuple-element.9.refs_5_.refs_0_, bf16[512,2048]{1,0:T(8,128)(2,1)} %bitcast.4.dy_ref.refs_6_.refs_7_.refs_8_.refs_9_.refs_1_.refs_2_.refs_3_.refs_4_, ...), custom_call_target="tpu_custom_call" | custom-call | flops 603979776 | bytes 2818048 | tf_op jit(solution)/shard_map/keep/pallas_call | solution.py:113
  169.2 1.7 add_convert_fusion.3
  171.0 0.1 collective-permute-start.1
  171.2 1.7 add_convert_fusion.2
  173.0 2.6 %collective-permute-start.5 = (bf16[576,512]{1,0:T(8,128)(2,1)S(1)}, bf16[576,512]{1,0:T(8,128)(2,1)S(1)}, u32[]{:S(2)}, u32[]{:S(2)}) collective-permute-start(bf16[576,512]{1,0:T(8,128)(2,1)S(1)} %broadcast_select_fusion.2), channel_id=1, source_target_pairs={{0,64},{16,80},{32,96},{48,112},{64,0},{80,16},{96,32},{112,48},{1... | collective-permute-start | bytes 1769480 | tf_op jit(solution)/shard_map/ppermute | solution.py:240
  175.6 1.7 add_convert_fusion.1
  177.4 1.1 collective-permute-start.9
  178.5 1.7 add_convert_fusion
  180.4 6.3 %collective-permute-done.1 = bf16[576,512]{1,0:T(8,128)(2,1)S(1)} collective-permute-done((bf16[576,512]{1,0:T(8,128)(2,1)S(1)}, bf16[576,512]{1,0:T(8,128)(2,1)S(1)}, u32[]{:S(2)}, u32[]{:S(2)}) %collective-permute-start.1) | collective-permute-done | bytes 589856 | tf_op jit(solution)/shard_map/ppermute | solution.py:240
  186.7 0.2 add_convert_fusion.7
  187.1 0.8 collective-permute-start.2
  187.8 1.3 collective-permute-done.5
  189.2 0.2 add_convert_fusion.6
  189.4 1.1 collective-permute-start.6
  190.6 3.8 %collective-permute-done.9 = bf16[576,512]{1,0:T(8,128)(2,1)S(1)} collective-permute-done((bf16[576,512]{1,0:T(8,128)(2,1)S(1)}, bf16[576,512]{1,0:T(8,128)(2,1)S(1)}, u32[]{:S(2)}, u32[]{:S(2)}) %collective-permute-start.9) | collective-permute-done | bytes 589856 | tf_op jit(solution)/shard_map/ppermute | solution.py:240
  194.4 0.2 add_convert_fusion.5
  194.8 1.8 collective-permute-done.13
  196.7 0.2 add_convert_fusion.4
  197.0 1.6 collective-permute-start.14
  198.6 2.9 %collective-permute-done.2 = bf16[576,256]{1,0:T(8,128)(2,1)S(1)} collective-permute-done((bf16[576,256]{1,0:T(8,128)(2,1)S(1)}, bf16[576,256]{1,0:T(8,128)(2,1)S(1)}, u32[]{:S(2)}, u32[]{:S(2)}) %collective-permute-start.2) | collective-permute-done | bytes 294944 | tf_op jit(solution)/shard_map/ppermute | solution.py:240
  201.5 0.1 add_convert_fusion.11
  201.7 2.3 %collective-permute-start.3 = (bf16[576,128]{1,0:T(8,128)(2,1)S(1)}, bf16[576,128]{1,0:T(8,128)(2,1)S(1)}, u32[]{:S(2)}, u32[]{:S(2)}) collective-permute-start(bf16[576,128]{1,0:T(8,128)(2,1)S(1)} %broadcast_select_fusion.11), channel_id=1, source_target_pairs={{0,48},{16,32},{32,16},{48,0},{64,112},{80,96},{96,80},{112,64},{1... | collective-permute-start | bytes 442376 | tf_op jit(solution)/shard_map/ppermute | solution.py:240
  203.9 0.1 add_convert_fusion.10
  204.2 0.1 add_convert_fusion.9
  204.4 1.6 collective-permute-start.11
  205.9 0.1 add_convert_fusion.8
  206.1 1.0 collective-permute-start.15
  207.1 1.0 collective-permute-done.3
  208.2 1.2 collective-permute-done.7
  209.4 0.2 collective-permute-done.11
  209.7 1.7 collective-permute-done.15
  211.5 0.9 copy.22
  212.4 0.8 copy.23
  213.2 3.1 %convolution_convert_fusion.2 = bf16[160,2048]{1,0:T(8,128)(2,1)} fusion(bf16[512,2048]{1,0:T(8,128)(2,1)} %bitcast.11, s32[160]{0:T(256)S(1)} %multiply_add_fusion), kind=kOutput, calls=%fused_computation.3 | convolution fusion | flops 335953920 | bytes 2753152 | tf_op jit(solution)/shard_map/dot_general | solution.py:231
  (70 shorter events, 2.2 us)
Async XLA Ops:
  0.6 1.6 copy-start
  4.3 8.7 %copy-start.9 = (bf16[160,2048]{1,0:T(8,128)(2,1)S(1)}, bf16[160,2048]{1,0:T(8,128)(2,1)}, u32[]{:S(2)}) copy-start(bf16[160,2048]{1,0:T(8,128)(2,1)} %param.14) | copy-start | bytes 1966084
  4.3 57.9 %all-to-all-start.1 = ((bf16[16,32,2048]{2,1,0:T(8,128)(2,1)}), bf16[16,32,2048]{2,1,0:T(8,128)(2,1)S(1)}, u32[]{:S(2)}, u32[]{:S(2)}) async-start(bf16[16,32,2048]{2,1,0:T(8,128)(2,1)} %bitcast.61), calls=%async_computation.1 | async-start | bytes 4194304 | tf_op jit(solution)/shard_map/all_to_all | solution.py:188
  62.2 5.0 %copy-start.13 = (s32[2]{0:T(128)S(1)}, s32[2]{0:T(128)}, u32[]{:S(2)}) copy-start(s32[2]{0:T(128)} %constant.73) | copy-start | bytes 28
  62.2 54.2 %all-to-all-start = ((bf16[16,32,2048]{2,1,0:T(8,128)(2,1)}), bf16[16,32,2048]{2,1,0:T(8,128)(2,1)}, u32[]{:S(2)}, u32[]{:S(2)}) async-start(bf16[16,32,2048]{2,1,0:T(8,128)(2,1)} %bitcast.60), calls=%async_computation | async-start | bytes 4194304 | tf_op jit(solution)/shard_map/all_to_all | solution.py:188
  116.3 1.4 copy-start.6
  117.7 1.4 copy-start.7
  123.9 2.8 %copy-start.2 = (bf16[2,768,512]{2,1,0:T(8,128)(2,1)}, bf16[2,768,512]{2,1,0:T(8,128)(2,1)S(1)}, u32[]{:S(2)}) copy-start(bf16[2,768,512]{2,1,0:T(8,128)(2,1)S(1)} %dgate_up.1) | copy-start | bytes 4718596
  123.9 3.4 %copy-start.12 = (s32[2]{0:T(128)S(1)}, s32[2]{0:T(128)}, u32[]{:S(2)}) copy-start(s32[2]{0:T(128)} %constant.74) | copy-start | bytes 28
  123.9 3.7 %copy-start.10 = (s32[2]{0:T(128)S(1)}, s32[2]{0:T(128)}, u32[]{:S(2)}) copy-start(s32[2]{0:T(128)} %constant.65.clone) | copy-start | bytes 28
  123.9 3.7 %copy-start.11 = (s32[2]{0:T(128)S(1)}, s32[2]{0:T(128)}, u32[]{:S(2)}) copy-start(s32[2]{0:T(128)} %constant.66.clone) | copy-start | bytes 28
  126.7 42.5 %collective-permute-start = (bf16[576,1024]{1,0:T(8,128)(2,1)}, bf16[576,1024]{1,0:T(8,128)(2,1)}, u32[]{:S(2)}, u32[]{:S(2)}) collective-permute-start(bf16[576,1024]{1,0:T(8,128)(2,1)} %give.4), channel_id=1, source_target_pairs={{0,64},{16,80},{32,96},{48,112},{64,0},{80,16},{96,32},{112,48},{1... | collective-permute-start | bytes 3538952 | tf_op jit(solution)/shard_map/ppermute | solution.py:223
  128.0 1.4 copy-start.3
  132.1 39.0 %collective-permute-start.4 = (bf16[576,1024]{1,0:T(8,128)(2,1)}, bf16[576,1024]{1,0:T(8,128)(2,1)}, u32[]{:S(2)}, u32[]{:S(2)}) collective-permute-start(bf16[576,1024]{1,0:T(8,128)(2,1)} %give.5), channel_id=1, source_target_pairs={{0,192},{16,208},{32,224},{48,240},{64,128},{80,144},{96,160},{112... | collective-permute-start | bytes 3538952 | tf_op jit(solution)/shard_map/ppermute | solution.py:223
  138.0 7.3 %copy-start.4 = (bf16[2,768,512]{2,1,0:T(8,128)(2,1)S(1)}, bf16[2,768,512]{2,1,0:T(8,128)(2,1)}, u32[]{:S(2)}) copy-start(bf16[2,768,512]{2,1,0:T(8,128)(2,1)} %copy-done.2) | copy-start | bytes 4718596
  138.0 37.6 %collective-permute-start.8 = (bf16[576,1024]{1,0:T(8,128)(2,1)}, bf16[576,1024]{1,0:T(8,128)(2,1)}, u32[]{:S(2)}, u32[]{:S(2)}) collective-permute-start(bf16[576,1024]{1,0:T(8,128)(2,1)} %give.6), channel_id=1, source_target_pairs={{0,16},{16,0},{32,48},{48,32},{64,80},{80,64},{96,112},{112,96},{1... | collective-permute-start | bytes 3538952 | tf_op jit(solution)/shard_map/ppermute | solution.py:223
  143.1 35.4 %collective-permute-start.12 = (bf16[576,1024]{1,0:T(8,128)(2,1)}, bf16[576,1024]{1,0:T(8,128)(2,1)}, u32[]{:S(2)}, u32[]{:S(2)}) collective-permute-start(bf16[576,1024]{1,0:T(8,128)(2,1)} %give.7), channel_id=1, source_target_pairs={{0,48},{16,32},{32,16},{48,0},{64,112},{80,96},{96,80},{112,64},{1... | collective-permute-start | bytes 3538952 | tf_op jit(solution)/shard_map/ppermute | solution.py:223
  151.8 1.4 copy-start.8
  153.2 60.0 %all-to-all-start.2 = ((bf16[16,32,2048]{2,1,0:T(8,128)(2,1)}), bf16[16,32,2048]{2,1,0:T(8,128)(2,1)}, u32[]{:S(2)}, u32[]{:S(2)}) async-start(bf16[16,32,2048]{2,1,0:T(8,128)(2,1)} %bitcast.58), calls=%async_computation.2 | async-start | bytes 4194304 | tf_op jit(solution)/shard_map/all_to_all | solution.py:228
  158.0 1.4 copy-start.5
  171.0 15.7 %collective-permute-start.1 = (bf16[576,512]{1,0:T(8,128)(2,1)S(1)}, bf16[576,512]{1,0:T(8,128)(2,1)S(1)}, u32[]{:S(2)}, u32[]{:S(2)}) collective-permute-start(bf16[576,512]{1,0:T(8,128)(2,1)S(1)} %broadcast_select_fusion.3), channel_id=1, source_target_pairs={{0,192},{16,208},{32,224},{48,240},{64,128},{80,144},{96,160},{112... | collective-permute-start | bytes 1769480 | tf_op jit(solution)/shard_map/ppermute | solution.py:240
  173.0 16.2 %collective-permute-start.5 = (bf16[576,512]{1,0:T(8,128)(2,1)S(1)}, bf16[576,512]{1,0:T(8,128)(2,1)S(1)}, u32[]{:S(2)}, u32[]{:S(2)}) collective-permute-start(bf16[576,512]{1,0:T(8,128)(2,1)S(1)} %broadcast_select_fusion.2), channel_id=1, source_target_pairs={{0,64},{16,80},{32,96},{48,112},{64,0},{80,16},{96,32},{112,48},{1... | collective-permute-start | bytes 1769480 | tf_op jit(solution)/shard_map/ppermute | solution.py:240
  177.4 17.0 %collective-permute-start.9 = (bf16[576,512]{1,0:T(8,128)(2,1)S(1)}, bf16[576,512]{1,0:T(8,128)(2,1)S(1)}, u32[]{:S(2)}, u32[]{:S(2)}) collective-permute-start(bf16[576,512]{1,0:T(8,128)(2,1)S(1)} %broadcast_select_fusion.1), channel_id=1, source_target_pairs={{0,48},{16,32},{32,16},{48,0},{64,112},{80,96},{96,80},{112,64},{1... | collective-permute-start | bytes 1769480 | tf_op jit(solution)/shard_map/ppermute | solution.py:240
  180.3 16.3 %collective-permute-start.13 = (bf16[576,512]{1,0:T(8,128)(2,1)S(1)}, bf16[576,512]{1,0:T(8,128)(2,1)S(1)}, u32[]{:S(2)}, u32[]{:S(2)}) collective-permute-start(bf16[576,512]{1,0:T(8,128)(2,1)S(1)} %broadcast_select_fusion), channel_id=1, source_target_pairs={{0,16},{16,0},{32,48},{48,32},{64,80},{80,64},{96,112},{112,96},{1... | collective-permute-start | bytes 1769480 | tf_op jit(solution)/shard_map/ppermute | solution.py:240
  187.1 14.4 %collective-permute-start.2 = (bf16[576,256]{1,0:T(8,128)(2,1)S(1)}, bf16[576,256]{1,0:T(8,128)(2,1)S(1)}, u32[]{:S(2)}, u32[]{:S(2)}) collective-permute-start(bf16[576,256]{1,0:T(8,128)(2,1)S(1)} %broadcast_select_fusion.7), channel_id=1, source_target_pairs={{0,16},{16,0},{32,48},{48,32},{64,80},{80,64},{96,112},{112,96},{1... | collective-permute-start | bytes 884744 | tf_op jit(solution)/shard_map/ppermute | solution.py:240
  189.4 14.5 %collective-permute-start.6 = (bf16[576,256]{1,0:T(8,128)(2,1)S(1)}, bf16[576,256]{1,0:T(8,128)(2,1)S(1)}, u32[]{:S(2)}, u32[]{:S(2)}) collective-permute-start(bf16[576,256]{1,0:T(8,128)(2,1)S(1)} %broadcast_select_fusion.6), channel_id=1, source_target_pairs={{0,48},{16,32},{32,16},{48,0},{64,112},{80,96},{96,80},{112,64},{1... | collective-permute-start | bytes 884744 | tf_op jit(solution)/shard_map/ppermute | solution.py:240
  194.7 9.4 %collective-permute-start.10 = (bf16[576,256]{1,0:T(8,128)(2,1)S(1)}, bf16[576,256]{1,0:T(8,128)(2,1)S(1)}, u32[]{:S(2)}, u32[]{:S(2)}) collective-permute-start(bf16[576,256]{1,0:T(8,128)(2,1)S(1)} %broadcast_select_fusion.5), channel_id=1, source_target_pairs={{0,64},{16,80},{32,96},{48,112},{64,0},{80,16},{96,32},{112,48},{1... | collective-permute-start | bytes 884744 | tf_op jit(solution)/shard_map/ppermute | solution.py:240
  197.0 9.0 %collective-permute-start.14 = (bf16[576,256]{1,0:T(8,128)(2,1)S(1)}, bf16[576,256]{1,0:T(8,128)(2,1)S(1)}, u32[]{:S(2)}, u32[]{:S(2)}) collective-permute-start(bf16[576,256]{1,0:T(8,128)(2,1)S(1)} %broadcast_select_fusion.4), channel_id=1, source_target_pairs={{0,192},{16,208},{32,224},{48,240},{64,128},{80,144},{96,160},{112... | collective-permute-start | bytes 884744 | tf_op jit(solution)/shard_map/ppermute | solution.py:240
  201.7 6.4 %collective-permute-start.3 = (bf16[576,128]{1,0:T(8,128)(2,1)S(1)}, bf16[576,128]{1,0:T(8,128)(2,1)S(1)}, u32[]{:S(2)}, u32[]{:S(2)}) collective-permute-start(bf16[576,128]{1,0:T(8,128)(2,1)S(1)} %broadcast_select_fusion.11), channel_id=1, source_target_pairs={{0,48},{16,32},{32,16},{48,0},{64,112},{80,96},{96,80},{112,64},{1... | collective-permute-start | bytes 442376 | tf_op jit(solution)/shard_map/ppermute | solution.py:240
  204.1 5.2 %collective-permute-start.7 = (bf16[576,128]{1,0:T(8,128)(2,1)S(1)}, bf16[576,128]{1,0:T(8,128)(2,1)S(1)}, u32[]{:S(2)}, u32[]{:S(2)}) collective-permute-start(bf16[576,128]{1,0:T(8,128)(2,1)S(1)} %broadcast_select_fusion.10), channel_id=1, source_target_pairs={{0,16},{16,0},{32,48},{48,32},{64,80},{80,64},{96,112},{112,96},{1... | collective-permute-start | bytes 442376 | tf_op jit(solution)/shard_map/ppermute | solution.py:240
  204.4 5.2 %collective-permute-start.11 = (bf16[576,128]{1,0:T(8,128)(2,1)S(1)}, bf16[576,128]{1,0:T(8,128)(2,1)S(1)}, u32[]{:S(2)}, u32[]{:S(2)}) collective-permute-start(bf16[576,128]{1,0:T(8,128)(2,1)S(1)} %broadcast_select_fusion.9), channel_id=1, source_target_pairs={{0,192},{16,208},{32,224},{48,240},{64,128},{80,144},{96,160},{112... | collective-permute-start | bytes 442376 | tf_op jit(solution)/shard_map/ppermute | solution.py:240
  206.1 5.2 %collective-permute-start.15 = (bf16[576,128]{1,0:T(8,128)(2,1)S(1)}, bf16[576,128]{1,0:T(8,128)(2,1)S(1)}, u32[]{:S(2)}, u32[]{:S(2)}) collective-permute-start(bf16[576,128]{1,0:T(8,128)(2,1)S(1)} %broadcast_select_fusion.8), channel_id=1, source_target_pairs={{0,64},{16,80},{32,96},{48,112},{64,0},{80,16},{96,32},{112,48},{1... | collective-permute-start | bytes 442376 | tf_op jit(solution)/shard_map/ppermute | solution.py:240
  213.2 3.1 %copy-start.1 = (bf16[160,2048]{1,0:T(8,128)(2,1)S(1)}, bf16[160,2048]{1,0:T(8,128)(2,1)}, u32[]{:S(2)}) copy-start(bf16[160,2048]{1,0:T(8,128)(2,1)} %param.13) | copy-start | bytes 1966084

commit v4 on v3

v4 whole, which is shorter than its diff:
```python
import jax
import jax.numpy as jnp
from jax import lax
from jax.experimental import pallas as pl
from jax.experimental.pallas import tpu as pltpu
from jax.sharding import PartitionSpec as P

SLOTS = 32
SIDE = 4
LANE = 128
CHUNKS = 4


def slot_table(routed, num_experts):
    rows = routed.shape[0]
    places = jnp.arange(rows, dtype=jnp.int32)
    same = (routed[:, None] == routed[None, :]) & (places[:, None] < places[None, :])
    slots = jnp.sum(same.astype(jnp.int32), axis=0)
    target = routed * SLOTS + slots
    spots = jnp.arange(num_experts * SLOTS, dtype=jnp.int32)
    return (spots[:, None] == target[None, :]).astype(jnp.bfloat16)


def feature_blocks(ref, table, f, chunk):
    pair = [
        ref[:, pl.ds(pl.multiple_of(table[f, 2 * chunk + k] * LANE, LANE), LANE)] for k in range(2)
    ]
    return jnp.concatenate(pair, axis=1)


def product(left, right):
    return jnp.dot(left, right, preferred_element_type=jnp.float32).astype(jnp.bfloat16)


def dgate_up_kernel(table, w_ref, dy_ref, a_ref, s_ref, hid_ref, out_ref, give_ref):
    step = pl.program_id(0)
    last = pl.num_programs(0) - 1
    start = hid_ref.shape[0] - give_ref.shape[0]
    for chunk in range(CHUNKS):

        @pl.when(step == jnp.minimum(chunk, last))
        def _():
            give_ref[:, 2 * LANE * chunk : 2 * LANE * (chunk + 1)] = product(
                hid_ref[start:, :], feature_blocks(dy_ref, table, 3, chunk)
            )

    dhidden = lax.dot_general(
        w_ref[...], dy_ref[...], (((1,), (1,)), ((), ())), preferred_element_type=jnp.float32
    )
    out_ref[0] = (dhidden * a_ref[...]).astype(jnp.bfloat16)
    out_ref[1] = (dhidden * s_ref[...]).astype(jnp.bfloat16)


def make_dgate_up(table, w_out_t, rows_dy, slope, silu, hidden):
    ff, width = w_out_t.shape
    rows = rows_dy.shape[0]
    tile = 256
    per = 3 * ff // 4
    return pl.pallas_call(
        dgate_up_kernel,
        grid_spec=pltpu.PrefetchScalarGridSpec(
            num_scalar_prefetch=1,
            grid=(ff // tile,),
            in_specs=[
                pl.BlockSpec((tile, width), lambda i, t: (i, 0)),
                pl.BlockSpec((rows, width), lambda i, t: (0, 0)),
                pl.BlockSpec((tile, rows), lambda i, t: (i, 0)),
                pl.BlockSpec((tile, rows), lambda i, t: (i, 0)),
                pl.BlockSpec((ff, rows), lambda i, t: (0, 0)),
            ],
            out_specs=[
                pl.BlockSpec((2, tile, rows), lambda i, t: (0, i, 0)),
                pl.BlockSpec((per, 2 * CHUNKS * LANE), lambda i, t: (0, 0)),
            ],
        ),
        out_shape=[
            jax.ShapeDtypeStruct((2, ff, rows), jnp.bfloat16),
            jax.ShapeDtypeStruct((per, 2 * CHUNKS * LANE), jnp.bfloat16),
        ],
        compiler_params=pltpu.CompilerParams(vmem_limit_bytes=24 * 1024 * 1024),
        cost_estimate=pl.CostEstimate(
            flops=2 * ff * rows * width + 4 * per * rows * CHUNKS * LANE,
            bytes_accessed=12 * ff * rows + 4 * rows * width + 4 * per * CHUNKS * LANE,
            transcendentals=0,
        ),
        name="dgate_up",
    )(table, w_out_t, rows_dy, slope, silu, hidden)


def partials_kernel(flows, table, dgu_ref, hid_ref, x_ref, dy_ref, *outs):
    per = outs[0].shape[0]
    split = dgu_ref.shape[0]
    for out, f in zip(outs, flows):
        low, high = f * per, (f + 1) * per
        for chunk in range(CHUNKS):
            to = slice(2 * LANE * chunk, 2 * LANE * (chunk + 1))
            if low < split:
                end = min(high, split)
                out[: end - low, to] = product(dgu_ref[low:end, :], feature_blocks(x_ref, table, f, chunk))
            if high > split:
                begin = max(low, split)
                out[begin - low :, to] = product(
                    hid_ref[begin - split : high - split, :], feature_blocks(dy_ref, table, f, chunk)
                )


def make_partials(flows, table, dgu, hidden, rows_x, rows_dy, name):
    rows = rows_x.shape[0]
    per = (dgu.shape[0] + hidden.shape[0]) // 4
    size = (per, 2 * CHUNKS * LANE)
    whole = pl.BlockSpec(memory_space=pltpu.VMEM)
    return pl.pallas_call(
        lambda *refs: partials_kernel(flows, *refs),
        in_specs=[pl.BlockSpec(memory_space=pltpu.SMEM)] + [whole] * 4,
        out_specs=[whole] * len(flows),
        out_shape=[jax.ShapeDtypeStruct(size, jnp.bfloat16)] * len(flows),
        compiler_params=pltpu.CompilerParams(vmem_limit_bytes=24 * 1024 * 1024),
        cost_estimate=pl.CostEstimate(
            flops=2 * len(flows) * per * rows * size[1],
            bytes_accessed=2 * (dgu.size + hidden.size + 2 * rows_x.size + len(flows) * per * size[1]),
            transcendentals=0,
        ),
        name=name,
    )(table, dgu, hidden, rows_x, rows_dy)


def pair_perm(axis, odd):
    def mate(i):
        return (3 - i) if odd else (i ^ 1)

    return [
        (x * SIDE + y, mate(x) * SIDE + y if axis == 0 else x * SIDE + mate(y))
        for x in range(SIDE)
        for y in range(SIDE)
    ]


FLOWS = ((0, False), (0, True), (1, False), (1, True))


def first_table(at, axis, odd):
    i = at[axis]
    minor = jnp.arange(SIDE, dtype=jnp.int32)

    def blocks(a, b):
        major = jnp.array([a, b], jnp.int32)
        ids = major[:, None] * SIDE + minor[None, :] if axis == 0 else minor[None, :] * SIDE + major[:, None]
        return ids.reshape(-1)

    low, high = (blocks(0, 1), blocks(2, 3)) if odd else (blocks(0, 3), blocks(1, 2))
    mine_low = (i < 2) if odd else ((i == 0) | (i == 3))
    return jnp.where(mine_low, high, low), jnp.where(mine_low, low, high)


def halves(block, at, axis, odd, step):
    i = at[axis]
    n = block.shape[1]
    if step % 2 == 1:
        low, high = block[:, : n // 2], block[:, n // 2 :]
        mine_low = (i % 2 == 0) if odd else (i < 2)
    else:
        q = n // 4
        if odd:
            low, high = block[:, : 2 * q], block[:, 2 * q :]
            mine_low = i < 2
        else:
            low = jnp.concatenate([block[:, :q], block[:, 3 * q :]], axis=1)
            high = block[:, q : 3 * q]
            mine_low = (i == 0) | (i == 3)
    return jnp.where(mine_low, high, low), jnp.where(mine_low, low, high)


def local(tokens, out_grads, expert_ids, w_gate_up, w_down_t):
    num_experts = lax.axis_size("expert")
    width = tokens.shape[1]
    ff = w_down_t.shape[2]
    rows = num_experts * SLOTS
    dispatch = slot_table(expert_ids[:, 0], num_experts)

    def send(values):
        slots = jnp.dot(dispatch, values, preferred_element_type=jnp.float32).astype(jnp.bfloat16)
        slots = slots.reshape(num_experts, SLOTS, width)
        got = lax.all_to_all(slots, "expert", split_axis=0, concat_axis=0, tiled=True)
        return got.reshape(rows, width)

    rows_x = send(tokens)
    rows_dy = send(out_grads)
    w_in = w_gate_up[0]
    w_out_t = w_down_t[0].T

    gate_up = lax.dot_general(
        w_in, rows_x, (((0,), (1,)), ((), ())), preferred_element_type=jnp.float32
    )
    gate = gate_up[:ff]
    upper = gate_up[ff:]
    sig = jax.nn.sigmoid(gate)
    silu = gate * sig
    hidden = (silu * upper).astype(jnp.bfloat16)
    slope = upper * sig * (1.0 + gate * (1.0 - sig))

    me = lax.axis_index("dp")
    at = (me // SIDE, me % SIDE)
    tables = [first_table(at, axis, odd) for axis, odd in FLOWS]

    to_give = jnp.stack([t[0] for t in tables])
    to_keep = jnp.stack([t[1] for t in tables])
    dgu, last_give = make_dgate_up(to_give, w_out_t, rows_dy, slope, silu, hidden)
    dgu = dgu.reshape(2 * ff, rows)
    gives = [*make_partials((0, 1, 2), to_give, dgu, hidden, rows_x, rows_dy, "give"), last_give]
    gots = [None] * 4
    for f in (3, 0, 1, 2):
        gots[f] = lax.ppermute(gives[f], "dp", pair_perm(*FLOWS[f]))
    drows = lax.dot_general(
        dgu, w_in, (((0,), (1,)), ((), ())), preferred_element_type=jnp.float32
    ).astype(jnp.bfloat16)
    keeps = make_partials((0, 1, 2, 3), to_keep, dgu, hidden, rows_x, rows_dy, "keep")
    blocks = [
        (keep.astype(jnp.float32) + got.astype(jnp.float32)).astype(jnp.bfloat16)
        for keep, got in zip(keeps, gots)
    ]

    returned = lax.all_to_all(
        drows.reshape(num_experts, SLOTS, width), "expert", split_axis=0, concat_axis=0, tiled=True
    ).reshape(rows, width)
    token_grads = lax.dot_general(
        dispatch, returned, (((0,), (0,)), ((), ())), preferred_element_type=jnp.float32
    ).astype(jnp.bfloat16)

    for step in range(1, 4):
        for f, (first_axis, first_odd) in enumerate(FLOWS):
            axis = first_axis if step < 2 else 1 - first_axis
            odd = first_odd if step % 2 == 0 else not first_odd
            give, keep = halves(blocks[f], at, axis, first_odd, step)
            got = lax.ppermute(give, "dp", pair_perm(axis, odd))
            blocks[f] = (keep.astype(jnp.float32) + got.astype(jnp.float32)).astype(jnp.bfloat16)
    summed = jnp.concatenate(blocks, axis=0).T
    return (token_grads, summed[None, :, : 2 * ff], summed[None, :, 2 * ff :])


def solution(mesh):
    return jax.shard_map(
        local,
        mesh=mesh,
        in_specs=(
            P(("dp", "expert"), None),
            P(("dp", "expert"), None),
            P(("dp", "expert"), None),
            P("expert", None, None),
            P("expert", None, None),
        ),
        out_specs=(P(("dp", "expert"), None), P("expert", "dp", None), P("expert", "dp", None)),
        check_vma=False,
    )
```

time: 218 us -> 227 us (1.041)
  Pallas kernels: 33.8 us -> 16.4 us
  waiting for transfers between devices: 104 us -> 118 us
  matrix products: 12.7 us -> 20.9 us
  starting transfers between devices: 37.4 us -> 44.3 us
  other arithmetic: 13.5 us -> 11 us
    ppermute x0 -> x4, waiting for transfers between devices: none -> 18.4 us  [local(): gots[f] = lax.ppermute(gives[f], 'dp', pair_perm(*FLOWS[f]))]
    pallas_call x10 -> x3, Pallas kernels: 33.8 us -> 16.4 us  [the longest x2 9.32 us: make_partials(): pl.pallas_call(lambda *refs: partials_kernel(flows, *refs), in_specs=[pl....]
    dot_general x0 -> x1, matrix products: none -> 7.56 us  [local(): lax.dot_general(dgu, w_in, (((0,), (1,)), ((), ())), preferred_element_ty...]
    ppermute x0 -> x4, starting transfers between devices: none -> 6.64 us  [local(): gots[f] = lax.ppermute(gives[f], 'dp', pair_perm(*FLOWS[f]))]
    ppermute x16 -> x12, waiting for transfers between devices: 20.2 us -> 15.8 us  [local(): got = lax.ppermute(give, 'dp', pair_perm(axis, odd))]
    convert_element_type x16, other arithmetic: 8.57 us -> 6.11 us  [local(): (keep.astype(jnp.float32) + got.astype(jnp.float32)).astype(jnp.bfloat16)]
    unnamed x31 -> x43, local copies, waits for them, and re-layouts: 13.5 us -> 12.4 us
    ppermute x16 -> x12, starting transfers between devices: 18.9 us -> 18.9 us  [local(): got = lax.ppermute(give, 'dp', pair_perm(axis, odd))]
  transfers between devices with their start and end apart: 19 -> 19, of which waited for: 11 -> 11; matrix products, arithmetic and copies ran while one was open for 12% -> 14% of each run, Pallas kernels for 12% -> 4%
where the time goes in v4:
time: 227 us; the launch traced here: 224 us
  waiting for transfers between devices  118 us (52%)
  starting transfers between devices  44.3 us (20%)
  matrix products  20.9 us (9%)
  Pallas kernels  16.4 us (7%)
  local copies, waits for them, and re-layouts  13.2 us (6%)
  other arithmetic  11 us (5%)
    all_to_all x2, waiting for transfers between devices, send(): lax.all_to_all(slots, 'expert', split_axis=0, concat_axis=0, tiled=True)  83.3 us
    ppermute x12, starting transfers between devices, local(): got = lax.ppermute(give, 'dp', pair_perm(axis, odd))  18.9 us
    ppermute x4, waiting for transfers between devices, local(): gots[f] = lax.ppermute(gives[f], 'dp', pair_perm(*FLOWS[f]))  18.4 us
    ppermute x12, waiting for transfers between devices, local(): got = lax.ppermute(give, 'dp', pair_perm(axis, odd))  15.8 us
    all_to_all x2, starting transfers between devices, send(): lax.all_to_all(slots, 'expert', split_axis=0, concat_axis=0, tiled=True)  13.6 us
    unnamed x43, local copies, waits for them, and re-layouts  12.4 us
    pallas_call x2, Pallas kernels, make_partials(): pl.pallas_call(lambda *refs: partials_kernel(flows, *refs), in_specs=[pl....  9.32 us
    dot_general x1, matrix products, local(): lax.dot_general(dgu, w_in, (((0,), (1,)), ((), ())), preferred_element_ty...  7.56 us
  transfers between devices with their start and end apart: 19, of which 11 were waited for; matrix products, arithmetic and copies ran while one was open for 14% of the time, Pallas kernels for 4%

profile of v4, /device:TPU:2, one launch (start us, length us, event | category | flops | bytes accessed | tf_op | source)
XLA Modules:
  0.0 224.4 jit_solution(7123149809276057197)
XLA Ops:
  0.6 0.9 convert_reduce_fusion
  1.5 0.7 multiply_add_fusion
  2.2 2.0 convolution_convert_fusion
  4.2 8.7 %all-to-all-start.1 = ((bf16[16,32,2048]{2,1,0:T(8,128)(2,1)}), bf16[16,32,2048]{2,1,0:T(8,128)(2,1)S(1)}, u32[]{:S(2)}, u32[]{:S(2)}) async-start(bf16[16,32,2048]{2,1,0:T(8,128)(2,1)} %bitcast.41), calls=%async_computation.1 | async-start | bytes 4194304 | tf_op jit(solution)/shard_map/all_to_all | solution.py:183
  13.0 2.1 convolution_convert_fusion.1
  15.0 47.1 %all-to-all-done.1 = bf16[16,32,2048]{2,1,0:T(8,128)(2,1)S(1)} async-done(((bf16[16,32,2048]{2,1,0:T(8,128)(2,1)}), bf16[16,32,2048]{2,1,0:T(8,128)(2,1)S(1)}, u32[]{:S(2)}, u32[]{:S(2)}) %all-to-all-start.1) | async-done | bytes 2097184 | tf_op jit(solution)/shard_map/all_to_all | solution.py:183
  62.2 4.9 %all-to-all-start = ((bf16[16,32,2048]{2,1,0:T(8,128)(2,1)}), bf16[16,32,2048]{2,1,0:T(8,128)(2,1)}, u32[]{:S(2)}, u32[]{:S(2)}) async-start(bf16[16,32,2048]{2,1,0:T(8,128)(2,1)} %bitcast.40), calls=%async_computation | async-start | bytes 4194304 | tf_op jit(solution)/shard_map/all_to_all | solution.py:183
  67.8 3.2 %copy.20 = bf16[1,2048,768]{1,2,0:T(8,128)(2,1)S(1)} copy(bf16[1,2048,768]{2,1,0:T(8,128)(2,1)} %param.17) | data formatting | bytes 6291456 | tf_op args[4]
  71.3 6.3 %fusion.4 = f32[1536,512]{1,0:T(8,128)S(1)} fusion(bf16[512,2048]{1,0:T(8,128)(2,1)} %bitcast.34, bf16[1,2048,1536]{2,1,0:T(8,128)(2,1)} %param.16), kind=kOutput, calls=%fused_computation.4 | convolution fusion | flops 3221225472 | bytes 11534336 | tf_op jit(solution)/shard_map/dot_general | solution.py:191
  77.6 2.5 %multiply_convert_fusion = (bf16[768,512]{1,0:T(8,128)(2,1)}, f32[768,512]{1,0:T(8,128)}, f32[768,512]{1,0:T(8,128)}) fusion(f32[1536,512]{1,0:T(8,128)S(1)} %fusion.4), kind=kLoop, calls=%fused_computation.13 | loop fusion | flops 4325376 | bytes 7077888 | tf_op jit(solution)/shard_map/convert_element_type | solution.py:198
  80.1 36.2 %all-to-all-done = bf16[16,32,2048]{2,1,0:T(8,128)(2,1)} async-done(((bf16[16,32,2048]{2,1,0:T(8,128)(2,1)}), bf16[16,32,2048]{2,1,0:T(8,128)(2,1)}, u32[]{:S(2)}, u32[]{:S(2)}) %all-to-all-start) | async-done | bytes 2097184 | tf_op jit(solution)/shard_map/all_to_all | solution.py:183
  116.3 1.4 copy-done.2
  117.8 1.4 copy-done.3
  119.2 1.1 copy-done.4
  120.3 7.1 %dgate_up.1 = (bf16[2,768,512]{2,1,0:T(8,128)(2,1)S(1)}, bf16[576,1024]{1,0:T(8,128)(2,1)}) custom-call(s32[4,8]{1,0:T(4,128)S(1)} %pad_add_fusion.table.refs_0_, bf16[768,2048]{1,0:T(8,128)(2,1)S(1)} %bitcast.33, bf16[512,2048]{1,0:T(8,128)(2,1)} %bitcast.4.dy_ref.refs_4_, f32[768,512]{1,0:T(8,128)S(1)} %copy-done.2, f32[768,512]{1,0:T(8,128)S(1)} %copy-done.3, ...), custom_call_target="tpu_custom_call" | custom-call | flops 2214592512 | bytes 10092544 | tf_op jit(solution)/shard_map/dgate_up/pallas_call | solution.py:59
  127.4 3.0 %collective-permute-start.12 = (bf16[576,1024]{1,0:T(8,128)(2,1)}, bf16[576,1024]{1,0:T(8,128)(2,1)}, u32[]{:S(2)}, u32[]{:S(2)}) collective-permute-start(bf16[576,1024]{1,0:T(8,128)(2,1)} %get-tuple-element.20), channel_id=1, source_target_pairs={{0,48},{16,32},{32,16},{48,0},{64,112},{80,96},{96,80},{112,64},{1... | collective-permute-start | bytes 3538952 | tf_op jit(solution)/shard_map/ppermute | solution.py:212
  130.4 4.8 %give.1 = (bf16[576,1024]{1,0:T(8,128)(2,1)S(1)}, bf16[576,1024]{1,0:T(8,128)(2,1)S(1)}, bf16[576,1024]{1,0:T(8,128)(2,1)}) custom-call(s32[4,8]{1,0:T(4,128)S(1)} %pad_add_fusion.table.refs_0_, bf16[1536,512]{1,0:T(8,128)(2,1)S(1)} %bitcast.37, bf16[768,512]{1,0:T(8,128)(2,1)S(1)} %copy-done.5, bf16[512,2048]{1,0:T(8,128)(2,1)S(1)} %bitcast.35, ...), custom_call_target="tpu_custom_call" | custom-call | flops 1811939328 | bytes 10092544 | tf_op jit(solution)/shard_map/give/pallas_call | solution.py:112
  135.2 1.0 copy-done.12
  136.3 1.0 copy-done.14
  137.3 0.2 collective-permute-start.8
  137.5 7.6 %fusion.7 = bf16[512,2048]{1,0:T(8,128)(2,1)} fusion(bf16[1536,512]{1,0:T(8,128)(2,1)S(1)} %bitcast.38, bf16[1,2048,1536]{2,1,0:T(8,128)(2,1)} %param.16), kind=kOutput, calls=%fused_computation.7 | convolution fusion | flops 3222274048 | bytes 9961472 | tf_op jit(solution)/shard_map/dot_general | solution.py:213
  145.0 5.0 %all-to-all-start.2 = ((bf16[16,32,2048]{2,1,0:T(8,128)(2,1)}), bf16[16,32,2048]{2,1,0:T(8,128)(2,1)}, u32[]{:S(2)}, u32[]{:S(2)}) async-start(bf16[16,32,2048]{2,1,0:T(8,128)(2,1)} %bitcast.42), calls=%async_computation.2 | async-start | bytes 4194304 | tf_op jit(solution)/shard_map/all_to_all | solution.py:222
  150.1 1.6 collective-permute-start.4
  151.7 1.4 copy-done.11
  153.1 4.5 %keep.1 = (bf16[576,1024]{1,0:T(8,128)(2,1)S(1)}, bf16[576,1024]{1,0:T(8,128)(2,1)S(1)}, bf16[576,1024]{1,0:T(8,128)(2,1)S(1)}, bf16[576,1024]{1,0:T(8,128)(2,1)S(1)}) custom-call(s32[4,8]{1,0:T(4,128)S(1)} %pad_add_fusion.1.refs_0_, bf16[1536,512]{1,0:T(8,128)(2,1)S(1)} %bitcast.39, bf16[768,512]{1,0:T(8,128)(2,1)S(1)} %copy-done.6, ...), custom_call_target="tpu_custom_call" | custom-call | flops 2415919104 | bytes 11272192 | tf_op jit(solution)/shard_map/keep/pallas_call | solution.py:112
  157.6 1.9 collective-permute-start
  159.5 1.7 add_convert_fusion
  161.3 2.0 collective-permute-start.13
  163.3 3.2 %collective-permute-done.8 = bf16[576,1024]{1,0:T(8,128)(2,1)} collective-permute-done((bf16[576,1024]{1,0:T(8,128)(2,1)}, bf16[576,1024]{1,0:T(8,128)(2,1)}, u32[]{:S(2)}, u32[]{:S(2)}) %collective-permute-start.8) | collective-permute-done | bytes 1179680 | tf_op jit(solution)/shard_map/ppermute | solution.py:212
  166.5 1.7 add_convert_fusion.1
  168.3 0.6 collective-permute-start.9
  168.9 9.6 %collective-permute-done.4 = bf16[576,1024]{1,0:T(8,128)(2,1)S(1)} collective-permute-done((bf16[576,1024]{1,0:T(8,128)(2,1)}, bf16[576,1024]{1,0:T(8,128)(2,1)S(1)}, u32[]{:S(2)}, u32[]{:S(2)}) %collective-permute-start.4) | collective-permute-done | bytes 1179680 | tf_op jit(solution)/shard_map/ppermute | solution.py:212
  178.5 0.5 add_convert_fusion.2
  179.1 1.8 collective-permute-start.5
  180.9 5.6 %collective-permute-done = bf16[576,1024]{1,0:T(8,128)(2,1)S(1)} collective-permute-done((bf16[576,1024]{1,0:T(8,128)(2,1)S(1)}, bf16[576,1024]{1,0:T(8,128)(2,1)S(1)}, u32[]{:S(2)}, u32[]{:S(2)}) %collective-permute-start) | collective-permute-done | bytes 1179680 | tf_op jit(solution)/shard_map/ppermute | solution.py:212
  186.5 0.5 add_convert_fusion.3
  187.1 0.6 collective-permute-start.1
  187.7 0.2 add_convert_fusion.4
  188.0 1.6 collective-permute-start.14
  189.5 0.2 add_convert_fusion.5
  189.8 0.1 broadcast_select_fusion.5
  189.9 3.1 %collective-permute-start.10 = (bf16[576,256]{1,0:T(8,128)(2,1)S(1)}, bf16[576,256]{1,0:T(8,128)(2,1)S(1)}, u32[]{:S(2)}, u32[]{:S(2)}) collective-permute-start(bf16[576,256]{1,0:T(8,128)(2,1)S(1)} %broadcast_select_fusion.5), channel_id=1, source_target_pairs={{0,64},{16,80},{32,96},{48,112},{64,0},{80,16},{96,32},{112,48},{1... | collective-permute-start | bytes 884744 | tf_op jit(solution)/shard_map/ppermute | solution.py:234
  193.0 6.1 %collective-permute-done.5 = bf16[576,512]{1,0:T(8,128)(2,1)S(1)} collective-permute-done((bf16[576,512]{1,0:T(8,128)(2,1)S(1)}, bf16[576,512]{1,0:T(8,128)(2,1)S(1)}, u32[]{:S(2)}, u32[]{:S(2)}) %collective-permute-start.5) | collective-permute-done | bytes 589856 | tf_op jit(solution)/shard_map/ppermute | solution.py:234
  199.2 0.2 add_convert_fusion.6
  199.4 1.3 collective-permute-start.6
  200.7 2.7 %collective-permute-done.1 = bf16[576,512]{1,0:T(8,128)(2,1)S(1)} collective-permute-done((bf16[576,512]{1,0:T(8,128)(2,1)S(1)}, bf16[576,512]{1,0:T(8,128)(2,1)S(1)}, u32[]{:S(2)}, u32[]{:S(2)}) %collective-permute-start.1) | collective-permute-done | bytes 589856 | tf_op jit(solution)/shard_map/ppermute | solution.py:234
  203.4 0.2 add_convert_fusion.7
  203.7 0.1 broadcast_select_fusion.7
  203.8 2.0 collective-permute-start.2
  205.8 1.3 collective-permute-done.14
  207.1 0.1 add_convert_fusion.8
  207.3 3.2 %collective-permute-start.15 = (bf16[576,128]{1,0:T(8,128)(2,1)S(1)}, bf16[576,128]{1,0:T(8,128)(2,1)S(1)}, u32[]{:S(2)}, u32[]{:S(2)}) collective-permute-start(bf16[576,128]{1,0:T(8,128)(2,1)S(1)} %broadcast_select_fusion.8), channel_id=1, source_target_pairs={{0,64},{16,80},{32,96},{48,112},{64,0},{80,16},{96,32},{112,48},{1... | collective-permute-start | bytes 442376 | tf_op jit(solution)/shard_map/ppermute | solution.py:234
  210.5 0.1 add_convert_fusion.9
  210.6 0.1 collective-permute-start.11
  210.8 0.1 add_convert_fusion.10
  210.9 2.0 collective-permute-start.7
  212.9 0.1 add_convert_fusion.11
  213.1 0.6 collective-permute-start.3
  213.8 2.1 collective-permute-done.11
  215.9 0.2 collective-permute-done.7
  216.2 3.3 %collective-permute-done.3 = bf16[576,128]{1,0:T(8,128)(2,1)S(1)} collective-permute-done((bf16[576,128]{1,0:T(8,128)(2,1)S(1)}, bf16[576,128]{1,0:T(8,128)(2,1)S(1)}, u32[]{:S(2)}, u32[]{:S(2)}) %collective-permute-start.3) | collective-permute-done | bytes 147488 | tf_op jit(solution)/shard_map/ppermute | solution.py:234
  219.7 0.9 copy.22
  220.6 0.8 copy.23
  221.4 3.0 %convolution_convert_fusion.2 = bf16[160,2048]{1,0:T(8,128)(2,1)} fusion(bf16[512,2048]{1,0:T(8,128)(2,1)} %bitcast.11, s32[160]{0:T(256)S(1)} %multiply_add_fusion), kind=kOutput, calls=%fused_computation.8 | convolution fusion | flops 335953920 | bytes 2753152 | tf_op jit(solution)/shard_map/dot_general | solution.py:225
  (78 shorter events, 1.8 us)
Async XLA Ops:
  0.6 1.6 copy-start
  4.2 8.7 %copy-start.15 = (bf16[160,2048]{1,0:T(8,128)(2,1)S(1)}, bf16[160,2048]{1,0:T(8,128)(2,1)}, u32[]{:S(2)}) copy-start(bf16[160,2048]{1,0:T(8,128)(2,1)} %param.14) | copy-start | bytes 1966084
  4.2 57.9 %all-to-all-start.1 = ((bf16[16,32,2048]{2,1,0:T(8,128)(2,1)}), bf16[16,32,2048]{2,1,0:T(8,128)(2,1)S(1)}, u32[]{:S(2)}, u32[]{:S(2)}) async-start(bf16[16,32,2048]{2,1,0:T(8,128)(2,1)} %bitcast.41), calls=%async_computation.1 | async-start | bytes 4194304 | tf_op jit(solution)/shard_map/all_to_all | solution.py:183
  62.1 5.6 %copy-start.7 = (bf16[16,32,2048]{2,1,0:T(8,128)(2,1)}, bf16[16,32,2048]{2,1,0:T(8,128)(2,1)S(1)}, u32[]{:S(2)}) copy-start(bf16[16,32,2048]{2,1,0:T(8,128)(2,1)S(1)} %all-to-all-done.1) | copy-start | bytes 6291460
  62.1 5.0 %copy-start.16 = (s32[2]{0:T(128)S(1)}, s32[2]{0:T(128)}, u32[]{:S(2)}) copy-start(s32[2]{0:T(128)} %constant.65.clone) | copy-start | bytes 28
  62.1 5.1 %copy-start.17 = (s32[2]{0:T(128)S(1)}, s32[2]{0:T(128)}, u32[]{:S(2)}) copy-start(s32[2]{0:T(128)} %constant.66.clone) | copy-start | bytes 28
  62.1 5.3 %copy-start.19 = (s32[2]{0:T(128)S(1)}, s32[2]{0:T(128)}, u32[]{:S(2)}) copy-start(s32[2]{0:T(128)} %constant.74) | copy-start | bytes 28
  62.1 5.5 %copy-start.18 = (s32[2]{0:T(128)S(1)}, s32[2]{0:T(128)}, u32[]{:S(2)}) copy-start(s32[2]{0:T(128)} %constant.72) | copy-start | bytes 28
  62.2 54.2 %all-to-all-start = ((bf16[16,32,2048]{2,1,0:T(8,128)(2,1)}), bf16[16,32,2048]{2,1,0:T(8,128)(2,1)}, u32[]{:S(2)}, u32[]{:S(2)}) async-start(bf16[16,32,2048]{2,1,0:T(8,128)(2,1)} %bitcast.40), calls=%async_computation | async-start | bytes 4194304 | tf_op jit(solution)/shard_map/all_to_all | solution.py:183
  116.3 1.4 copy-start.2
  117.7 1.4 copy-start.3
  119.2 1.1 copy-start.4
  120.3 10.1 %copy-start.5 = (bf16[768,512]{1,0:T(8,128)(2,1)S(1)}, bf16[768,512]{1,0:T(8,128)(2,1)}, u32[]{:S(2)}) copy-start(bf16[768,512]{1,0:T(8,128)(2,1)} %get-tuple-element.27.hid_ref.refs_2_) | copy-start | bytes 2359300
  120.3 10.1 %copy-start.8 = (bf16[16,32,2048]{2,1,0:T(8,128)(2,1)S(1)}, bf16[16,32,2048]{2,1,0:T(8,128)(2,1)}, u32[]{:S(2)}) copy-start(bf16[16,32,2048]{2,1,0:T(8,128)(2,1)} %copy-done.7) | copy-start | bytes 6291460
  127.4 10.1 %copy-start.10 = (bf16[2,768,512]{2,1,0:T(8,128)(2,1)}, bf16[2,768,512]{2,1,0:T(8,128)(2,1)S(1)}, u32[]{:S(2)}) copy-start(bf16[2,768,512]{2,1,0:T(8,128)(2,1)S(1)} %get-tuple-element.12) | copy-start | bytes 4718596
  127.4 32.1 %collective-permute-start.12 = (bf16[576,1024]{1,0:T(8,128)(2,1)}, bf16[576,1024]{1,0:T(8,128)(2,1)}, u32[]{:S(2)}, u32[]{:S(2)}) collective-permute-start(bf16[576,1024]{1,0:T(8,128)(2,1)} %get-tuple-element.20), channel_id=1, source_target_pairs={{0,48},{16,32},{32,16},{48,0},{64,112},{80,96},{96,80},{112,64},{1... | collective-permute-start | bytes 3538952 | tf_op jit(solution)/shard_map/ppermute | solution.py:212
  135.2 1.0 copy-start.12
  136.3 1.0 copy-start.14
  137.3 29.2 %collective-permute-start.8 = (bf16[576,1024]{1,0:T(8,128)(2,1)}, bf16[576,1024]{1,0:T(8,128)(2,1)}, u32[]{:S(2)}, u32[]{:S(2)}) collective-permute-start(bf16[576,1024]{1,0:T(8,128)(2,1)} %get-tuple-element.18), channel_id=1, source_target_pairs={{0,16},{16,0},{32,48},{48,32},{64,80},{80,64},{96,112},{112,96},{1... | collective-permute-start | bytes 3538952 | tf_op jit(solution)/shard_map/ppermute | solution.py:212
  145.0 6.6 %copy-start.6 = (bf16[768,512]{1,0:T(8,128)(2,1)S(1)}, bf16[768,512]{1,0:T(8,128)(2,1)}, u32[]{:S(2)}) copy-start(bf16[768,512]{1,0:T(8,128)(2,1)} %get-tuple-element.27.hid_ref.refs_2_) | copy-start | bytes 2359300
  145.0 6.6 %copy-start.9 = (bf16[16,32,2048]{2,1,0:T(8,128)(2,1)S(1)}, bf16[16,32,2048]{2,1,0:T(8,128)(2,1)}, u32[]{:S(2)}) copy-start(bf16[16,32,2048]{2,1,0:T(8,128)(2,1)} %copy-done.7) | copy-start | bytes 6291460
  145.0 76.4 %all-to-all-start.2 = ((bf16[16,32,2048]{2,1,0:T(8,128)(2,1)}), bf16[16,32,2048]{2,1,0:T(8,128)(2,1)}, u32[]{:S(2)}, u32[]{:S(2)}) async-start(bf16[16,32,2048]{2,1,0:T(8,128)(2,1)} %bitcast.42), calls=%async_computation.2 | async-start | bytes 4194304 | tf_op jit(solution)/shard_map/all_to_all | solution.py:222
  150.1 28.4 %collective-permute-start.4 = (bf16[576,1024]{1,0:T(8,128)(2,1)}, bf16[576,1024]{1,0:T(8,128)(2,1)S(1)}, u32[]{:S(2)}, u32[]{:S(2)}) collective-permute-start(bf16[576,1024]{1,0:T(8,128)(2,1)} %copy-done.14), channel_id=1, source_target_pairs={{0,192},{16,208},{32,224},{48,240},{64,128},{80,144},{96,160},{112... | collective-permute-start | bytes 3538952 | tf_op jit(solution)/shard_map/ppermute | solution.py:212
  151.7 1.4 copy-start.11
  153.1 4.5 %copy-start.13 = (bf16[576,1024]{1,0:T(8,128)(2,1)S(1)}, bf16[576,1024]{1,0:T(8,128)(2,1)}, u32[]{:S(2)}) copy-start(bf16[576,1024]{1,0:T(8,128)(2,1)} %copy-done.12) | copy-start | bytes 3538948
  157.6 28.9 %collective-permute-start = (bf16[576,1024]{1,0:T(8,128)(2,1)S(1)}, bf16[576,1024]{1,0:T(8,128)(2,1)S(1)}, u32[]{:S(2)}, u32[]{:S(2)}) collective-permute-start(bf16[576,1024]{1,0:T(8,128)(2,1)S(1)} %copy-done.13), channel_id=1, source_target_pairs={{0,64},{16,80},{32,96},{48,112},{64,0},{80,16},{96,32},{112,48},{1... | collective-permute-start | bytes 3538952 | tf_op jit(solution)/shard_map/ppermute | solution.py:212
  161.3 26.4 %collective-permute-start.13 = (bf16[576,512]{1,0:T(8,128)(2,1)S(1)}, bf16[576,512]{1,0:T(8,128)(2,1)S(1)}, u32[]{:S(2)}, u32[]{:S(2)}) collective-permute-start(bf16[576,512]{1,0:T(8,128)(2,1)S(1)} %broadcast_select_fusion), channel_id=1, source_target_pairs={{0,16},{16,0},{32,48},{48,32},{64,80},{80,64},{96,112},{112,96},{1... | collective-permute-start | bytes 1769480 | tf_op jit(solution)/shard_map/ppermute | solution.py:234
  168.3 21.3 %collective-permute-start.9 = (bf16[576,512]{1,0:T(8,128)(2,1)S(1)}, bf16[576,512]{1,0:T(8,128)(2,1)S(1)}, u32[]{:S(2)}, u32[]{:S(2)}) collective-permute-start(bf16[576,512]{1,0:T(8,128)(2,1)S(1)} %broadcast_select_fusion.1), channel_id=1, source_target_pairs={{0,48},{16,32},{32,16},{48,0},{64,112},{80,96},{96,80},{112,64},{1... | collective-permute-start | bytes 1769480 | tf_op jit(solution)/shard_map/ppermute | solution.py:234
  179.1 20.1 %collective-permute-start.5 = (bf16[576,512]{1,0:T(8,128)(2,1)S(1)}, bf16[576,512]{1,0:T(8,128)(2,1)S(1)}, u32[]{:S(2)}, u32[]{:S(2)}) collective-permute-start(bf16[576,512]{1,0:T(8,128)(2,1)S(1)} %broadcast_select_fusion.2), channel_id=1, source_target_pairs={{0,64},{16,80},{32,96},{48,112},{64,0},{80,16},{96,32},{112,48},{1... | collective-permute-start | bytes 1769480 | tf_op jit(solution)/shard_map/ppermute | solution.py:234
  187.1 16.4 %collective-permute-start.1 = (bf16[576,512]{1,0:T(8,128)(2,1)S(1)}, bf16[576,512]{1,0:T(8,128)(2,1)S(1)}, u32[]{:S(2)}, u32[]{:S(2)}) collective-permute-start(bf16[576,512]{1,0:T(8,128)(2,1)S(1)} %broadcast_select_fusion.3), channel_id=1, source_target_pairs={{0,192},{16,208},{32,224},{48,240},{64,128},{80,144},{96,160},{112... | collective-permute-start | bytes 1769480 | tf_op jit(solution)/shard_map/ppermute | solution.py:234
  188.0 19.2 %collective-permute-start.14 = (bf16[576,256]{1,0:T(8,128)(2,1)S(1)}, bf16[576,256]{1,0:T(8,128)(2,1)S(1)}, u32[]{:S(2)}, u32[]{:S(2)}) collective-permute-start(bf16[576,256]{1,0:T(8,128)(2,1)S(1)} %broadcast_select_fusion.4), channel_id=1, source_target_pairs={{0,192},{16,208},{32,224},{48,240},{64,128},{80,144},{96,160},{112... | collective-permute-start | bytes 884744 | tf_op jit(solution)/shard_map/ppermute | solution.py:234
  189.9 20.6 %collective-permute-start.10 = (bf16[576,256]{1,0:T(8,128)(2,1)S(1)}, bf16[576,256]{1,0:T(8,128)(2,1)S(1)}, u32[]{:S(2)}, u32[]{:S(2)}) collective-permute-start(bf16[576,256]{1,0:T(8,128)(2,1)S(1)} %broadcast_select_fusion.5), channel_id=1, source_target_pairs={{0,64},{16,80},{32,96},{48,112},{64,0},{80,16},{96,32},{112,48},{1... | collective-permute-start | bytes 884744 | tf_op jit(solution)/shard_map/ppermute | solution.py:234
  199.4 11.3 %collective-permute-start.6 = (bf16[576,256]{1,0:T(8,128)(2,1)S(1)}, bf16[576,256]{1,0:T(8,128)(2,1)S(1)}, u32[]{:S(2)}, u32[]{:S(2)}) collective-permute-start(bf16[576,256]{1,0:T(8,128)(2,1)S(1)} %broadcast_select_fusion.6), channel_id=1, source_target_pairs={{0,48},{16,32},{32,16},{48,0},{64,112},{80,96},{96,80},{112,64},{1... | collective-permute-start | bytes 884744 | tf_op jit(solution)/shard_map/ppermute | solution.py:234
  203.8 9.1 %collective-permute-start.2 = (bf16[576,256]{1,0:T(8,128)(2,1)S(1)}, bf16[576,256]{1,0:T(8,128)(2,1)S(1)}, u32[]{:S(2)}, u32[]{:S(2)}) collective-permute-start(bf16[576,256]{1,0:T(8,128)(2,1)S(1)} %broadcast_select_fusion.7), channel_id=1, source_target_pairs={{0,16},{16,0},{32,48},{48,32},{64,80},{80,64},{96,112},{112,96},{1... | collective-permute-start | bytes 884744 | tf_op jit(solution)/shard_map/ppermute | solution.py:234
  207.3 6.4 %collective-permute-start.15 = (bf16[576,128]{1,0:T(8,128)(2,1)S(1)}, bf16[576,128]{1,0:T(8,128)(2,1)S(1)}, u32[]{:S(2)}, u32[]{:S(2)}) collective-permute-start(bf16[576,128]{1,0:T(8,128)(2,1)S(1)} %broadcast_select_fusion.8), channel_id=1, source_target_pairs={{0,64},{16,80},{32,96},{48,112},{64,0},{80,16},{96,32},{112,48},{1... | collective-permute-start | bytes 442376 | tf_op jit(solution)/shard_map/ppermute | solution.py:234
  210.6 5.2 %collective-permute-start.11 = (bf16[576,128]{1,0:T(8,128)(2,1)S(1)}, bf16[576,128]{1,0:T(8,128)(2,1)S(1)}, u32[]{:S(2)}, u32[]{:S(2)}) collective-permute-start(bf16[576,128]{1,0:T(8,128)(2,1)S(1)} %broadcast_select_fusion.9), channel_id=1, source_target_pairs={{0,192},{16,208},{32,224},{48,240},{64,128},{80,144},{96,160},{112... | collective-permute-start | bytes 442376 | tf_op jit(solution)/shard_map/ppermute | solution.py:234
  210.9 5.2 %collective-permute-start.7 = (bf16[576,128]{1,0:T(8,128)(2,1)S(1)}, bf16[576,128]{1,0:T(8,128)(2,1)S(1)}, u32[]{:S(2)}, u32[]{:S(2)}) collective-permute-start(bf16[576,128]{1,0:T(8,128)(2,1)S(1)} %broadcast_select_fusion.10), channel_id=1, source_target_pairs={{0,16},{16,0},{32,48},{48,32},{64,80},{80,64},{96,112},{112,96},{1... | collective-permute-start | bytes 442376 | tf_op jit(solution)/shard_map/ppermute | solution.py:234
  213.1 6.4 %collective-permute-start.3 = (bf16[576,128]{1,0:T(8,128)(2,1)S(1)}, bf16[576,128]{1,0:T(8,128)(2,1)S(1)}, u32[]{:S(2)}, u32[]{:S(2)}) collective-permute-start(bf16[576,128]{1,0:T(8,128)(2,1)S(1)} %broadcast_select_fusion.11), channel_id=1, source_target_pairs={{0,48},{16,32},{32,16},{48,0},{64,112},{80,96},{96,80},{112,64},{1... | collective-permute-start | bytes 442376 | tf_op jit(solution)/shard_map/ppermute | solution.py:234
  220.6 3.8 %copy-start.1 = (bf16[160,2048]{1,0:T(8,128)(2,1)S(1)}, bf16[160,2048]{1,0:T(8,128)(2,1)}, u32[]{:S(2)}) copy-start(bf16[160,2048]{1,0:T(8,128)(2,1)} %param.13) | copy-start | bytes 1966084
